TPU v7x, 256 devices: a whole 4x4x8 slice. The times are simulated.
256 devices in a mesh: ctx: 32 (over z, y), head: 8 (over x, core).
Axes of the slice: x: 4, y: 4, z: 8, core: 2. Of those that a mesh axis runs over, the one named last changes fastest.
Arguments:
- latents: float32 [512, 1024], replicated, may hold values from -5 to 5
- observations: float32 [65536, 1024], P('ctx'), may hold values from -45 to 45
- w_query: float32 [1024, 1024], P(None, 'head'), as said below
- w_key: float32 [1024, 1024], P(None, 'head'), as said below
- w_value: float32 [1024, 1024], P(None, 'head'), may hold values from -0.1875 to 0.1875
- w_out: float32 [1024, 1024], P('head'), may hold values from -0.1875 to 0.1875
- d_out: float32 [512, 1024], replicated, may hold values from -6 to 6
Outputs:
- d_latents: float32 [512, 1024], P(None, 'head')
- d_observations: float32 [65536, 1024], P('ctx', 'head')
- d_w_query: float32 [1024, 1024], P(None, 'head')
- d_w_key: float32 [1024, 1024], P('ctx', 'head')
- d_w_value: float32 [1024, 1024], P('ctx', 'head')
- d_w_out: float32 [1024, 1024], P('head')
Inputs may be any that keep to these rules, and one draw needn't show every extreme that they name: `w_query`: every entry lies within -5 / sqrt(1024) to 5 / sqrt(1024). `w_key`: every entry lies within -7 / sqrt(1024) to 7 / sqrt(1024).
All inputs are finite; a program needn't handle non-finite values.
Results may differ from a plain program's by a relative error of at most 0.0003.
Values sent between devices are 32-bit elements; how exact they have to be, the bound alone decides.
No kernel may reach another device: no remote copies, remote signals or barrier semaphores. Data moves between devices by JAX's collectives and lax.ppermute only.
A program may use at most 128 MiB of HBM per device.

v0:
```python
import math

import jax
import jax.numpy as jnp
from jax import lax
from jax.sharding import PartitionSpec as P

DH = 128


def on_device(latents, observations, w_query, w_key, w_value, w_out, d_out):
    highest = lax.Precision.HIGHEST
    scale = 1.0 / math.sqrt(DH)
    lat_rows = latents.shape[0]
    tok_rows = observations.shape[0]
    width_here = w_query.shape[1]
    heads_here = width_here // DH
    queries = jnp.dot(
        latents, w_query, precision=highest, preferred_element_type=jnp.float32
    ).reshape(lat_rows, heads_here, DH)
    keys_here = jnp.dot(
        observations, w_key, precision=highest, preferred_element_type=jnp.float32
    ).reshape(tok_rows, heads_here, DH)
    values_here = jnp.dot(
        observations, w_value, precision=highest, preferred_element_type=jnp.float32
    ).reshape(tok_rows, heads_here, DH)
    scores = jnp.einsum("lhd,thd->hlt", queries, keys_here, precision=highest) * scale
    row_max = jnp.max(scores, axis=2)
    top = lax.pmax(row_max, "ctx")
    expo = jnp.exp(scores - top[..., None])
    total, accum = lax.psum(
        (jnp.sum(expo, axis=2), jnp.einsum("hlt,thd->hld", expo, values_here, precision=highest)),
        "ctx",
    )
    probs = expo / total[..., None]
    attended = accum / total[..., None]
    grad_flat = jnp.dot(d_out, w_out.T, precision=highest, preferred_element_type=jnp.float32)
    grad_heads = grad_flat.reshape(lat_rows, heads_here, DH)
    attended_flat = jnp.transpose(attended, (1, 0, 2)).reshape(lat_rows, width_here)
    d_w_out = jnp.dot(attended_flat.T, d_out, precision=highest, preferred_element_type=jnp.float32)
    dprobs = jnp.einsum("lhd,thd->hlt", grad_heads, values_here, precision=highest)
    delta = jnp.einsum("lhd,hld->hl", grad_heads, attended)
    dscores = probs * (dprobs - delta[..., None]) * scale
    dquery_part = jnp.einsum("hlt,thd->lhd", dscores, keys_here, precision=highest).reshape(
        lat_rows, width_here
    )
    dquery = lax.psum(dquery_part, "ctx")
    d_w_query = jnp.dot(latents.T, dquery, precision=highest, preferred_element_type=jnp.float32)
    latent_part = jnp.dot(dquery, w_query.T, precision=highest, preferred_element_type=jnp.float32)
    d_latents = lax.psum_scatter(latent_part, "head", scatter_dimension=1, tiled=True)
    dkey = jnp.einsum("hlt,lhd->thd", dscores, queries, precision=highest).reshape(
        tok_rows, width_here
    )
    dvalue = jnp.einsum("hlt,lhd->thd", probs, grad_heads, precision=highest).reshape(
        tok_rows, width_here
    )
    token_part = jnp.dot(
        dkey, w_key.T, precision=highest, preferred_element_type=jnp.float32
    ) + jnp.dot(dvalue, w_value.T, precision=highest, preferred_element_type=jnp.float32)
    d_observations = lax.psum_scatter(token_part, "head", scatter_dimension=1, tiled=True)
    joined = jnp.concatenate([dkey, dvalue], axis=1)
    own_rows = observations.shape[1] // lax.axis_size("ctx")
    full_grad = lax.psum(
        jnp.dot(observations.T, joined, precision=highest, preferred_element_type=jnp.float32),
        "ctx",
    )
    mine = lax.dynamic_slice_in_dim(full_grad, lax.axis_index("ctx") * own_rows, own_rows, 0)
    d_w_key = mine[:, :width_here]
    d_w_value = mine[:, width_here:]
    return (d_latents, d_observations, d_w_query, d_w_key, d_w_value, d_w_out)


def solution(mesh):
    placed = (
        P(),
        P("ctx", None),
        P(None, "head"),
        P(None, "head"),
        P(None, "head"),
        P("head", None),
        P(),
    )
    return jax.shard_map(
        on_device,
        mesh=mesh,
        in_specs=placed,
        out_specs=(
            P(None, "head"),
            P("ctx", "head"),
            P(None, "head"),
            P("ctx", "head"),
            P("ctx", "head"),
            P("head", None),
        ),
        check_vma=False,
    )
```

profile of v0, /device:TPU:1, one launch (start us, length us, event | category | flops | bytes accessed | tf_op | source)
XLA Modules:
  0.0 535.4 jit_solution(9107562078161389760)
XLA Ops:
  7.3 10.2 %fusion.20 = f32[2048,128]{1,0:T(8,128)S(1)} fusion(f32[2048,1024]{1,0:T(8,128)} %param.8, f32[1024,128]{1,0:T(8,128)} %param.10), kind=kOutput, calls=%fused_computation.28 | convolution fusion | flops 3221225472 | bytes 9961472 | tf_op jit(solution)/shard_map/dot_general | solution.py:21
  17.5 7.7 %fusion.22 = f32[2048,128]{1,0:T(8,128)} fusion(f32[2048,1024]{1,0:T(8,128)S(1)} %copy-done.1, f32[1024,128]{1,0:T(8,128)S(1)} %copy-done.8), kind=kOutput, calls=%fused_computation.30 | convolution fusion | flops 3221225472 | bytes 9961472 | tf_op jit(solution)/shard_map/dot_general | solution.py:24
  25.2 1.8 fusion.21
  27.0 5.2 multiply_reduce_fusion
  32.2 64.9 %pmax.7 = f32[512]{0:T(512)S(1)} all-reduce(f32[512]{0:T(512)S(1)} %get-tuple-element.16), channel_id=1, replica_groups=mesh['ctx'=32,'head'=8] {'ctx'}, use_global_device_ids=true, to_apply=%region_1.0 | all-reduce | flops 512 | bytes 4096 | tf_op jit(solution)/shard_map/pmax | solution.py:29
  97.2 7.0 %fusion.12 = f32[1,512,128]{2,1,0:T(8,128)} fusion(f32[2048,128]{1,0:T(8,128)} %fusion.22, f32[512,2048]{1,0:T(8,128)} %get-tuple-element.17, f32[512]{0:T(512)S(1)} %pmax.7), kind=kOutput, calls=%fused_computation.18 | convolution fusion | flops 1612709888 | bytes 5507072 | tf_op jit(solution)/shard_map/hlt,thd->hld/dot_general | solution.py:32
  104.2 3.0 fusion.2
  107.2 56.1 %psum.28 = f32[512]{0:T(512)S(1)} all-reduce(f32[512]{0:T(512)S(1)} %fusion.2), channel_id=1, replica_groups=mesh['ctx'=32,'head'=8] {'ctx'}, use_global_device_ids=true, to_apply=%region_3.0 | all-reduce | flops 512 | bytes 4096 | tf_op jit(solution)/shard_map/psum | solution.py:31
  163.3 89.5 %all-reduce.4.cloned.1.call-done = f32[1,512,128]{2,1,0:T(8,128)} async-done(((f32[1,512,128]{2,1,0:T(8,128)}), f32[1,512,128]{2,1,0:T(8,128)}) %all-reduce.4.cloned.1.call-update) | async-done | bytes 262160 | tf_op jit(solution)/shard_map/psum | solution.py:31
  252.9 3.0 fusion.15
  255.9 5.5 %convolution_bitcast_fusion = f32[2048,128]{0,1:T(8,128)S(1)} fusion(f32[512,128]{1,0:T(8,128)S(1)} %get-tuple-element.19, f32[512,2048]{1,0:T(8,128)} %get-tuple-element.17, f32[512]{0:T(512)S(1)} %psum.28, f32[512]{0:T(512)S(1)} %pmax.7), kind=kOutput, calls=%fused_computation.7 | convolution fusion | flops 1613758464 | bytes 5509120 | tf_op jit(solution)/shard_map/hlt,lhd->thd/dot_general | solution.py:54
  261.4 4.4 multiply_multiply_fusion
  265.9 5.3 convolution_bitcast_fusion.3
  271.2 2.3 convolution_bitcast_fusion.1
  273.6 8.2 %fusion.9 = f32[1024,256]{0,1:T(8,128)} fusion(f32[2048,1024]{1,0:T(8,128)S(1)} %bitcast.59, f32[2048,128]{0,1:T(8,128)S(1)} %convolution_bitcast_fusion, f32[2048,128]{0,1:T(8,128)S(1)} %convolution_bitcast_fusion.1), kind=kOutput, calls=%fused_computation.15 | convolution fusion | flops 6442975232 | bytes 11534336 | tf_op jit(solution)/shard_map/dot_general | solution.py:64
  281.9 148.5 %all-reduce.6.cloned.1.call-done = (f32[512,128]{0,1:T(8,128)}, f32[1024,256]{0,1:T(8,128)}) async-done(((f32[512,128]{0,1:T(8,128)}, f32[1024,256]{0,1:T(8,128)}), (f32[512,128]{0,1:T(8,128)}, f32[1024,256]{0,1:T(8,128)})) %all-reduce.6.cloned.1.call-update) | async-done | bytes 1310736 | tf_op jit(solution)/shard_map/psum | solution.py:47
  430.4 4.3 fusion.23
  435.0 8.1 %fusion.24 = f32[2048,1024]{1,0:T(8,128)S(1)} fusion(f32[2048,128]{0,1:T(8,128)S(1)} %convolution_bitcast_fusion.1, f32[1024,128]{1,0:T(8,128)} %param.10), kind=kOutput, calls=%fused_computation.32 | convolution fusion | flops 3221225472 | bytes 9961472 | tf_op jit(solution)/shard_map/dot_general | solution.py:57
  443.1 9.9 %convolution_add_fusion = f32[2048,1024]{1,0:T(8,128)} fusion(f32[2048,1024]{1,0:T(8,128)S(1)} %fusion.24, f32[2048,128]{0,1:T(8,128)S(1)} %copy-done.7, f32[1024,128]{1,0:T(8,128)S(1)} %copy-done.9), kind=kOutput, calls=%fused_computation | convolution fusion | flops 3223322624 | bytes 18350080 | tf_op jit(solution)/shard_map/dot_general | solution.py:59
  454.0 2.2 fusion.13
  456.3 1.3 convolution_bitcast_fusion.2
  457.5 1.0 copy.13
  460.9 8.6 %reduce-scatter.3.cloned.1.call-done = f32[512,128]{1,0:T(8,128)} async-done(((f32[512,1024]{1,0:T(8,128)}), f32[512,128]{1,0:T(8,128)}) %reduce-scatter.3.cloned.1.call-update) | async-done | bytes 262160 | tf_op jit(solution)/shard_map/reduce_scatter | solution.py:50
  469.5 59.1 %reduce-scatter.5.cloned.1.call-done = f32[2048,128]{1,0:T(8,128)} async-done(((f32[2048,1024]{1,0:T(8,128)}), f32[2048,128]{1,0:T(8,128)}) %reduce-scatter.5.cloned.1.call-update) | async-done | bytes 1048592 | tf_op jit(solution)/shard_map/reduce_scatter | solution.py:60
  (42 shorter events, 3.8 us)
Async XLA Ops:
  7.2 245.7 %copy-start = (f32[512,1024]{1,0:T(8,128)S(1)}, f32[512,1024]{1,0:T(8,128)}, u32[]{:S(2)}) copy-start(f32[512,1024]{1,0:T(8,128)} %param.13) | copy-start | bytes 6291460
  7.2 245.7 %all-reduce.4.cloned.1.call-start = ((), (), s32[]{:S(2)}) async-start(), calls=%async_computation.2 | async-start | bytes 524288 | tf_op jit(solution)/shard_map/psum | solution.py:31
  7.2 10.2 %copy-start.1 = (f32[2048,1024]{1,0:T(8,128)S(1)}, f32[2048,1024]{1,0:T(8,128)}, u32[]{:S(2)}) copy-start(f32[2048,1024]{1,0:T(8,128)} %param.8) | copy-start | bytes 25165828
  7.2 10.2 %copy-start.8 = (f32[1024,128]{1,0:T(8,128)S(1)}, f32[1024,128]{1,0:T(8,128)}, u32[]{:S(2)}) copy-start(f32[1024,128]{1,0:T(8,128)} %param.11) | copy-start | bytes 1572868
  17.4 7.8 %copy-start.3 = (f32[512,1024]{1,0:T(8,128)S(1)}, f32[512,1024]{1,0:T(8,128)}, u32[]{:S(2)}) copy-start(f32[512,1024]{1,0:T(8,128)} %param.7) | copy-start | bytes 6291460
  17.5 7.8 %copy-start.10 = (f32[1024,128]{1,0:T(8,128)S(1)}, f32[1024,128]{1,0:T(8,128)}, u32[]{:S(2)}) copy-start(f32[1024,128]{1,0:T(8,128)} %param.9) | copy-start | bytes 1572868
  104.1 326.2 %all-reduce.6.cloned.1.call-start = ((), (), s32[]{:S(2)}) async-start(), calls=%async_computation.5 | async-start | bytes 2621440 | tf_op jit(solution)/shard_map/psum | solution.py:47
  255.9 5.6 %copy-start.2 = (f32[512,2048]{1,0:T(8,128)S(1)}, f32[512,2048]{1,0:T(8,128)}, u32[]{:S(2)}) copy-start(f32[512,2048]{1,0:T(8,128)} %get-tuple-element.17) | copy-start | bytes 12582916
  255.9 5.6 %copy-start.5 = (f32[2048,128]{1,0:T(8,128)S(1)}, f32[2048,128]{1,0:T(8,128)}, u32[]{:S(2)}) copy-start(f32[2048,128]{1,0:T(8,128)} %fusion.22) | copy-start | bytes 3145732
  255.9 17.7 %slice-start = ((s8[8388608]{0:T(1024)(128)(4,1)}), s8[4194304]{0:T(1024)(128)(4,1)S(1)}, s32[]{:S(2)}) async-start(s8[8388608]{0:T(1024)(128)(4,1)} %bitcast.58), calls=%async_computation.6 | async-start | bytes 8388608
  261.4 12.1 %copy-start.6 = (f32[2048,128]{0,1:T(8,128)}, f32[2048,128]{0,1:T(8,128)S(1)}, u32[]{:S(2)}) copy-start(f32[2048,128]{0,1:T(8,128)S(1)} %convolution_bitcast_fusion) | copy-start | bytes 3145732
  261.4 12.1 %slice-start.1 = ((s8[8388608]{0:T(1024)(128)(4,1)}), s8[4194304]{0:T(1024)(128)(4,1)S(1)}, s32[]{:S(2)}) async-start(s8[8388608]{0:T(1024)(128)(4,1)} %bitcast.58), calls=%async_computation.7 | async-start | bytes 8388608
  281.8 187.7 %reduce-scatter.3.cloned.1.call-start = ((), (), s32[]{:S(2)}) async-start(), calls=%async_computation.3 | async-start | bytes 2359296 | tf_op jit(solution)/shard_map/reduce_scatter | solution.py:50
  434.7 93.9 %reduce-scatter.5.cloned.1.call-start = ((), (), s32[]{:S(2)}) async-start(), calls=%async_computation.4 | async-start | bytes 9437184 | tf_op jit(solution)/shard_map/reduce_scatter | solution.py:60
  435.0 8.1 %copy-start.7 = (f32[2048,128]{0,1:T(8,128)S(1)}, f32[2048,128]{0,1:T(8,128)}, u32[]{:S(2)}) copy-start(f32[2048,128]{0,1:T(8,128)} %copy-done.6) | copy-start | bytes 3145732
  435.0 8.1 %copy-start.9 = (f32[1024,128]{1,0:T(8,128)S(1)}, f32[1024,128]{1,0:T(8,128)}, u32[]{:S(2)}) copy-start(f32[1024,128]{1,0:T(8,128)} %param.11) | copy-start | bytes 1572868
  453.1 1.0 copy-start.11
  453.1 3.2 copy-start.12
  454.0 2.2 copy-start.4
Sparse Core Ops, SparseCore 0:
  104.3 148.5 all-reduce.3
  282.0 148.3 all-reduce.5
  434.8 34.6 reduce-scatter.2
  472.6 55.9 reduce-scatter.4
where the time goes:
time: 539 us; the launch traced here: 535 us
  waiting for transfers between devices  306 us (57%)
  blocking collectives  121 us (22%)
  matrix products  86.5 us (16%)
  between operations  14.3 us (3%)
    psum x1, waiting for transfers between devices, on_device(): dquery = lax.psum(dquery_part, 'ctx')  148 us
    psum x1, waiting for transfers between devices, on_device(): lax.psum((jnp.sum(expo, axis=2), jnp.einsum('hlt,thd->hld', expo, values_...  89.5 us
    pmax x1, blocking collectives, on_device(): top = lax.pmax(row_max, 'ctx')  64.9 us
    reduce_scatter x1, waiting for transfers between devices, on_device(): lax.psum_scatter(token_part, 'head', scatter_dimension=1, tiled=True)  59.1 us
    psum x1, blocking collectives, on_device(): lax.psum((jnp.sum(expo, axis=2), jnp.einsum('hlt,thd->hld', expo, values_...  56.1 us
  transfers between devices with their start and end apart: 4, of which 4 were waited for; matrix products, arithmetic and copies ran while one was open for 5% of the time, Pallas kernels for 0%

commit v1 on v0

v1 whole, which is shorter than its diff:
```python
import math

import jax
import jax.numpy as jnp
from jax import lax
from jax.experimental import pallas as pl
from jax.experimental.pallas import tpu as pltpu
from jax.sharding import PartitionSpec as P

DH = 128
NY = 4
CHUNK = 512
F32 = jnp.float32
BF16 = jnp.bfloat16
VMEM = pltpu.VMEM
WHOLE = pl.BlockSpec(memory_space=VMEM)
ANY = pl.BlockSpec(memory_space=pl.ANY)
HBM = pl.BlockSpec(memory_space=pltpu.HBM)
SCALARS = pl.BlockSpec(memory_space=pltpu.SMEM)


def shape(*dims, dtype=F32):
    return jax.ShapeDtypeStruct(dims, dtype)


def params(mib):
    return pltpu.CompilerParams(vmem_limit_bytes=mib << 20)


def cost(macs, bytes_accessed):
    return pl.CostEstimate(flops=6 * macs, bytes_accessed=bytes_accessed, transcendentals=0)


def mm(a, b, ca=1, cb=0):
    return lax.dot_general(a, b, (((ca,), (cb,)), ((), ())), preferred_element_type=F32)


def split(a):
    hi = a.astype(BF16)
    return hi, (a - hi.astype(F32)).astype(BF16)


def dot3(a, b, ca=1, cb=0):
    a_hi, a_lo = split(a)
    b_hi, b_lo = split(b)
    return mm(a_hi, b_hi, ca, cb) + mm(a_hi, b_lo, ca, cb) + mm(a_lo, b_hi, ca, cb)


def scores_of(kv_ref, q3, g3):
    hi_k, hi_v, lo_k, lo_v = (kv_ref[:, i * DH : (i + 1) * DH] for i in range(4))
    scores = mm(jnp.concatenate([hi_k, lo_k, hi_k], axis=1), q3[...], 1, 1)
    return scores, mm(jnp.concatenate([hi_v, lo_v, hi_v], axis=1), g3[...], 1, 1)


def forward_kernel(
    scale, core_ref, lat_hbm, dout_hbm, wq_hbm, wo_hbm, wk_hbm, wv_hbm, obs_hbm,
    kv_ref, q3, g3, sent_ref, stat_ref, given_ref,
    lat_v, dout_v, wq_v, wo_v, wk_v, wv_v, obs_v, sems, obs_sems, w_hi, w_lo,
):
    step = pl.program_id(0)
    loads = [
        pltpu.make_async_copy(source, target, sems.at[i])
        for i, (source, target) in enumerate(
            (
                (wk_hbm, wk_v), (wv_hbm, wv_v), (lat_hbm, lat_v),
                (wq_hbm, wq_v), (dout_hbm, dout_v), (wo_hbm, wo_v),
            )
        )
    ]

    def load_tokens(i):
        rows = pl.ds(pl.multiple_of(i * CHUNK, CHUNK), CHUNK)
        return pltpu.make_async_copy(obs_hbm.at[rows], obs_v.at[i], obs_sems.at[i])

    @pl.when(step == 0)
    def _():
        loads[0].start()
        loads[1].start()
        load_tokens(0).start()
        for load in loads[2:]:
            load.start()
        for i in range(1, obs_v.shape[0]):
            load_tokens(i).start()
        loads[0].wait()
        loads[1].wait()
        hi, lo = split(wk_v[...])
        w_hi[:, :DH], w_lo[:, :DH] = hi, lo
        hi, lo = split(wv_v[...])
        w_hi[:, DH:], w_lo[:, DH:] = hi, lo
        for d in range(given_ref.shape[0]):
            at = pl.ds(pl.multiple_of((2 * d + 1 - core_ref[0]) * DH, DH), DH)
            given_ref[d, :, :DH], given_ref[d, :, DH:] = wk_v[at], wv_v[at]

    load_tokens(step).wait()
    o_hi, o_lo = split(obs_v[step])
    kv = mm(o_hi, w_hi[...]) + mm(o_hi, w_lo[...]) + mm(o_lo, w_hi[...])
    hi, lo = split(kv)
    kv_ref[:, : 2 * DH], kv_ref[:, 2 * DH :] = hi, lo

    @pl.when(step == 0)
    def _():
        loads[2].wait()
        loads[3].wait()
        top, bottom = split(dot3(lat_v[...], wq_v[...]) * scale)
        q3[:, :DH], q3[:, DH : 2 * DH], q3[:, 2 * DH :] = top, top, bottom
        loads[4].wait()
        loads[5].wait()
        top, bottom = split(dot3(dout_v[...], wo_v[...], 1, 1))
        g3[:, :DH], g3[:, DH : 2 * DH], g3[:, 2 * DH :] = top, top, bottom

    scores, dprobs = scores_of(kv_ref, q3, g3)
    top = jnp.max(scores, axis=0, keepdims=True)
    expo = jnp.exp(scores - top)
    total = jnp.sum(expo, axis=0, keepdims=True)
    mix = jnp.sum(expo * dprobs, axis=0, keepdims=True)

    @pl.when(step == 0)
    def _():
        stat_ref[0:1], stat_ref[1:2], stat_ref[2:3] = top, total, mix

    @pl.when(step > 0)
    def _():
        before = stat_ref[0:1]
        now = jnp.maximum(before, top)
        w_before, w_new = jnp.exp(before - now), jnp.exp(top - now)
        stat_ref[0:1] = now
        stat_ref[1:2] = stat_ref[1:2] * w_before + total * w_new
        stat_ref[2:3] = stat_ref[2:3] * w_before + mix * w_new

    @pl.when(step == pl.num_programs(0) - 1)
    def _():
        sent_ref[...] = jnp.broadcast_to(stat_ref[...][None], sent_ref.shape)


def forward(n_ctx, core, latents, d_out, w_query, w_out, w_key, w_value, observations):
    lat, tok, width = latents.shape[0], observations.shape[0], observations.shape[1]
    steps = tok // CHUNK
    nx = width // DH // 2
    block = lambda cols: pl.BlockSpec((CHUNK, cols), lambda i: (i, 0))
    full = lambda *dims: pl.BlockSpec(dims, lambda i: (0,) * len(dims))
    return pl.pallas_call(
        lambda *refs: forward_kernel(1.0 / math.sqrt(DH), *refs),
        grid=(steps,),
        in_specs=[SCALARS] + [HBM] * 7,
        out_specs=[
            block(4 * DH), full(lat, 3 * DH), full(lat, 3 * DH),
            full(n_ctx, 3, lat), full(3, lat), full(nx, DH, 2 * DH),
        ],
        out_shape=[
            shape(tok, 4 * DH, dtype=BF16),
            shape(lat, 3 * DH, dtype=BF16), shape(lat, 3 * DH, dtype=BF16),
            shape(n_ctx, 3, lat), shape(3, lat), shape(nx, DH, 2 * DH),
        ],
        scratch_shapes=[
            VMEM(latents.shape, F32), VMEM(d_out.shape, F32), VMEM(w_query.shape, F32),
            VMEM(w_out.shape, F32), VMEM(w_key.shape, F32), VMEM(w_value.shape, F32),
            VMEM((steps, CHUNK, width), F32),
            pltpu.SemaphoreType.DMA((6,)), pltpu.SemaphoreType.DMA((steps,)),
            VMEM((width, 2 * DH), BF16), VMEM((width, 2 * DH), BF16),
        ],
        compiler_params=params(60),
        cost_estimate=cost(tok * width * 256 + 2 * tok * lat * DH, 18 << 20),
        name="forward",
    )(core, latents, d_out, w_query, w_out, w_key, w_value, observations)


def sums_kernel(y_ref, kv_ref, q3, g3, stat_ref, o0, o1, o2, o3, acc):
    step = pl.program_id(0)
    stat = stat_ref[...]
    shift = stat[2:3] / stat[1:2]
    scores, dprobs = scores_of(kv_ref, q3, g3)
    expo = jnp.exp(scores - stat[0:1])
    mixed = expo * (dprobs - shift)
    kv = kv_ref[...]
    hi, lo = kv[:, : 2 * DH], kv[:, 2 * DH :]
    e_hi, e_lo = split(expo)
    m_hi, m_lo = split(mixed)
    kv_sums = mm(hi, e_hi, 0, 0) + mm(lo, e_hi, 0, 0) + mm(hi, e_lo, 0, 0)
    k_hi, k_lo = hi[:, :DH], lo[:, :DH]
    ak_sums = mm(k_hi, m_hi, 0, 0) + mm(k_lo, m_hi, 0, 0) + mm(k_hi, m_lo, 0, 0)

    @pl.when(step == 0)
    def _():
        acc[:DH], acc[DH:] = ak_sums, kv_sums

    @pl.when(step > 0)
    def _():
        acc[:DH] += ak_sums
        acc[DH:] += kv_sums

    @pl.when(step == pl.num_programs(0) - 1)
    def _():
        rows = o0.shape[0]
        for k, out in enumerate((o0, o1, o2, o3)):
            at = lax.rem(y_ref[0] + k, NY) * rows
            out[...] = acc[:, pl.ds(pl.multiple_of(at, rows), rows)].T


def local_sums(y, kv, q3, g3, stat):
    tok, lat = kv.shape[0], q3.shape[0]
    block = lambda cols: pl.BlockSpec((CHUNK, cols), lambda i: (i, 0))
    rows = lat // NY
    return pl.pallas_call(
        sums_kernel,
        grid=(tok // CHUNK,),
        in_specs=[SCALARS, block(4 * DH), WHOLE, WHOLE, WHOLE],
        out_specs=[pl.BlockSpec((rows, 3 * DH), lambda i: (0, 0))] * NY,
        out_shape=[shape(rows, 3 * DH)] * NY,
        scratch_shapes=[VMEM((3 * DH, lat), F32)],
        compiler_params=params(24),
        cost_estimate=cost(3 * tok * lat * DH, 12 << 20),
        name="local_sums",
    )(y, kv, q3, g3, stat)


def grads_kernel(kv_ref, q3, g3, stat_ref, out_ref):
    stat = stat_ref[...]
    scores, dprobs = scores_of(kv_ref, q3, g3)
    probs = jnp.exp(scores - stat[0:1]) * stat[1:2]
    dscores = probs * (dprobs - stat[2:3])
    for at, value, packed in ((0, dscores, q3), (DH, probs, g3)):
        hi, lo = split(value)
        both = mm(hi, packed[:, DH:])
        out_ref[:, at : at + DH] = both[:, :DH] + both[:, DH:] + mm(lo, packed[:, :DH])


def token_grads(half, kv, q3, g3, stat):
    tok, lat = kv.shape[0], q3.shape[0]
    steps = tok // CHUNK // 2
    first = half * steps
    return pl.pallas_call(
        grads_kernel,
        grid=(steps,),
        in_specs=[
            pl.BlockSpec((CHUNK, 4 * DH), lambda i: (i + first, 0)), WHOLE, WHOLE, WHOLE,
        ],
        out_specs=pl.BlockSpec((CHUNK, 2 * DH), lambda i: (i, 0)),
        out_shape=shape(tok // 2, 2 * DH),
        compiler_params=params(24),
        cost_estimate=cost(2 * tok * lat * DH, 5 << 20),
        name="token_grads",
    )(kv, q3, g3, stat)


def project(own, other, w):
    o_hi, o_lo = split(own)
    t_hi, t_lo = split(other)
    hi = jnp.concatenate([o_hi, t_hi], axis=1)
    lo = jnp.concatenate([o_lo, t_lo], axis=1)
    both = mm(hi, w, 1, 1)
    return both[:, :DH] + both[:, DH:] + mm(lo, w[:DH], 1, 1)


def first_kernel(*refs):
    after, own_a, other_a, own_b, other_b, far, near, back, right_ref, left_ref = refs
    a, b = (own_a[...], other_a[...]), (own_b[...], other_b[...])
    right_ref[0] = project(*a, far[0])
    right_ref[1] = project(*b, near[0])
    left_ref[0] = project(*b, far[0])
    left_ref[1] = project(*a, back[0])


def second_kernel(after, own_a, other_a, own_b, other_b, near, back, ra, la, right_ref, left_ref):
    right_ref[...] = project(own_a[...], other_a[...], near[0]) + ra[0]
    left_ref[...] = project(own_b[...], other_b[...], back[0]) + la[0]


def token_part(kernel, a, b, w, which, after, extras, outs, name):
    rows = a[0].shape[0]
    block = pl.BlockSpec((CHUNK, 2 * DH), lambda i: (i, 0))
    pair = pl.BlockSpec((2, CHUNK, DH), lambda i: (0, i, 0))
    one = pl.BlockSpec((CHUNK, DH), lambda i: (i, 0))
    chosen = [pl.BlockSpec((1,) + w.shape[1:], lambda i, k=k: (k, 0, 0)) for k in which]
    return pl.pallas_call(
        kernel,
        grid=(rows // CHUNK,),
        in_specs=[ANY] + [block] * 4 + chosen
        + [pl.BlockSpec((1, CHUNK, DH), lambda i: (0, i, 0))] * len(extras),
        out_specs=[pair if len(o.shape) == 3 else one for o in outs],
        out_shape=outs,
        compiler_params=params(24),
        cost_estimate=cost(4 * rows * 4 * DH * DH, 6 << 20),
        name=name,
    )(after, *a, *b, *[w] * len(which), *extras)


def last_kernel(own_a, other_a, own_b, other_b, w, right1, left1, right2, left2, out_ref):
    step = pl.program_id(0)

    @pl.when(step < pl.num_programs(0) // 2)
    def _():
        out_ref[...] = project(own_a[...], other_a[...], w[0]) + right2[...] + left1[0]

    @pl.when(step >= pl.num_programs(0) // 2)
    def _():
        out_ref[...] = project(own_b[...], other_b[...], w[0]) + right1[0] + left2[...]


def token_last(a, b, w, right1, left1, right2, left2):
    rows = a[0].shape[0]
    steps = rows // CHUNK
    early = lambda i: jnp.minimum(i, steps - 1)
    late = lambda i: jnp.maximum(i - steps, 0)
    first = lambda cols: pl.BlockSpec((CHUNK, cols), lambda i: (early(i), 0))
    second = lambda cols: pl.BlockSpec((CHUNK, cols), lambda i: (late(i), 0))
    return pl.pallas_call(
        last_kernel,
        grid=(2 * steps,),
        in_specs=[
            first(2 * DH), first(2 * DH), second(2 * DH), second(2 * DH),
            pl.BlockSpec((1,) + w.shape[1:], lambda i: (0, 0, 0)),
            pl.BlockSpec((1, CHUNK, DH), lambda i: (1, late(i), 0)),
            pl.BlockSpec((1, CHUNK, DH), lambda i: (1, early(i), 0)),
            first(DH), second(DH),
        ],
        out_specs=pl.BlockSpec((CHUNK, DH), lambda i: (i, 0)),
        out_shape=shape(2 * rows, DH),
        compiler_params=params(24),
        cost_estimate=cost(2 * rows * 4 * DH * DH, 8 << 20),
        name="token_last",
    )(*a, *b, w, right1, left1, right2, left2)


def weights_kernel(after, y_ref, obs_ref, a_ref, b_ref, o0, o1, o2, o3, acc, blocks):
    step = pl.program_id(0)
    joined = jnp.where(step < pl.num_programs(0) // 2, a_ref[...], b_ref[...])
    j_hi, j_lo = split(joined)
    o_hi, o_lo = split(obs_ref[...])
    value = mm(j_hi, o_hi, 0, 0) + mm(j_lo, o_hi, 0, 0) + mm(j_hi, o_lo, 0, 0)

    @pl.when(step == 0)
    def _():
        acc[...] = value

    @pl.when(step > 0)
    def _():
        acc[...] += value

    @pl.when(step == pl.num_programs(0) - 1)
    def _():
        nz, own = o0.shape[0], o0.shape[1]
        for i in range(nz):
            group = acc[:, i * NY * own : (i + 1) * NY * own].T
            blocks[i] = group.reshape(NY, own, 2 * DH)
        for k, out in enumerate((o0, o1, o2, o3)):
            out[...] = blocks[:, lax.rem(y_ref[0] + k, NY)]


def weight_grads(dep, y, nz, observations, a, b):
    tok, width = observations.shape
    own = width // nz // NY
    steps = a.shape[0] // CHUNK
    return pl.pallas_call(
        weights_kernel,
        grid=(2 * steps,),
        in_specs=[
            ANY, SCALARS,
            pl.BlockSpec((CHUNK, width), lambda i: (i, 0)),
            pl.BlockSpec((CHUNK, 2 * DH), lambda i: (jnp.minimum(i, steps - 1), 0)),
            pl.BlockSpec((CHUNK, 2 * DH), lambda i: (jnp.maximum(i - steps, 0), 0)),
        ],
        out_specs=[pl.BlockSpec((nz, own, 2 * DH), lambda i: (0, 0, 0))] * NY,
        out_shape=[shape(nz, own, 2 * DH)] * NY,
        scratch_shapes=[VMEM((2 * DH, width), F32), VMEM((nz, NY, own, 2 * DH), F32)],
        compiler_params=params(24),
        cost_estimate=cost(tok * width * 2 * DH, 11 << 20),
        name="weight_grads",
    )(dep, y, observations, a, b)


def small_call(kernel, outs, operands, scalars, after=(), scratch=(), name=None):
    def body(*refs):
        kernel(*refs[len(after) :])

    return pl.pallas_call(
        body,
        in_specs=[ANY] * len(after) + [SCALARS] * len(scalars) + [WHOLE] * len(operands),
        out_specs=[WHOLE] * len(outs),
        out_shape=list(outs),
        scratch_shapes=list(scratch),
        compiler_params=params(24),
        cost_estimate=cost(1 << 20, 1 << 20),
        name=name,
    )(*after, *scalars, *operands)


def chip_weights_kernel(place_ref, wk_ref, wv_ref, taken_ref, out_ref):
    x, core = place_ref[0], place_ref[1]
    nx = out_ref.shape[0]
    for r in range(nx):
        d = lax.rem(x + r, nx)
        at = pl.ds(pl.multiple_of((2 * d + core) * DH, DH), DH)
        pieces = (wk_ref[at], wv_ref[at], taken_ref[d, :, :DH], taken_ref[d, :, DH:])
        for i, piece in enumerate(pieces):
            hi, lo = split(piece)
            cols = slice(i * DH, (i + 1) * DH)
            out_ref[r, :DH, cols], out_ref[r, DH:, cols] = hi, lo


def combine_kernel(stats_ref, stat_ref, shares_ref, deltas_ref):
    tops = stats_ref[:, 0, :]
    top = jnp.max(tops, axis=0, keepdims=True)
    weight = jnp.exp(tops - top)
    sums, mixes = stats_ref[:, 1, :], stats_ref[:, 2, :]
    total = jnp.sum(weight * sums, axis=0, keepdims=True)
    delta = jnp.sum(weight * mixes, axis=0, keepdims=True) / total
    stat_ref[0:1], stat_ref[1:2], stat_ref[2:3] = top, 1.0 / total, delta
    shares_ref[...] = (weight / total)[:, None]
    deltas_ref[...] = (mixes / sums - delta)[:, None]


def rows_kernel(scale, place_ref, shares_ref, deltas_ref, p0, p1, p2, p3, out_ref):
    z, y = place_ref[0], place_ref[1]
    rows = out_ref.shape[0]
    lanes = pl.ds(pl.multiple_of(y * rows, rows), rows)
    dq, att = 0.0, 0.0
    for k, part in enumerate((p0, p1, p2, p3)):
        source = z * NY + lax.rem(y + NY - k, NY)
        share = jnp.broadcast_to(shares_ref[source, :, lanes], (DH, rows)).T
        delta = jnp.broadcast_to(deltas_ref[source, :, lanes], (DH, rows)).T
        dq += share * (part[:, :DH] + delta * part[:, DH : 2 * DH])
        att += share * part[:, 2 * DH :]
    out_ref[:, :DH] = dq * scale
    out_ref[:, DH:] = att


def latent_part_kernel(both_ref, wq_ref, rows_ref, part_ref):
    rows = jnp.sum(both_ref[...], axis=0)
    rows_ref[...] = rows
    part = dot3(rows[:, :DH], wq_ref[...], 1, 1)
    for h in range(part_ref.shape[0]):
        part_ref[h] = part[:, h * DH : (h + 1) * DH]


def latent_rows_kernel(rows_ref, part_ref, w0, w1, w2, w3, out_ref):
    d_lat = jnp.sum(part_ref[...], axis=0)
    half = out_ref.shape[1]
    for i in range(out_ref.shape[0]):
        out_ref[i, :, : 2 * DH] = rows_ref[...]
        out_ref[i, :, 2 * DH : 3 * DH] = d_lat
        weights = (w0[i] + w1[i]) + (w2[i] + w3[i])
        out_ref[i, :, 3 * DH : 5 * DH] = weights[:half]
        out_ref[i, :, 5 * DH :] = weights[half:]


def gathered_kernel(got_ref, rows_ref, key_ref, value_ref):
    half = got_ref.shape[1]
    total = got_ref[0, :, 3 * DH :]
    for i in range(1, got_ref.shape[0]):
        total += got_ref[i, :, 3 * DH :]
    for i in range(got_ref.shape[0]):
        rows_ref[i * half : (i + 1) * half] = got_ref[i, :, : 3 * DH]
    key_ref[:half], key_ref[half:] = total[:, :DH], total[:, 2 * DH : 3 * DH]
    value_ref[:half], value_ref[half:] = total[:, DH : 2 * DH], total[:, 3 * DH :]


def final_kernel(y_ref, own, r1, r2, r3, lat_ref, dout_ref, d_lat_ref, d_wq_ref, d_wo_ref, both):
    rows = own.shape[0]
    for k, part in enumerate((own, r1, r2, r3)):
        at = pl.ds(pl.multiple_of(lax.rem(y_ref[0] + NY - k, NY) * rows, rows), rows)
        both[at] = part[:, : 2 * DH]
        d_lat_ref[at] = part[:, 2 * DH :]
    d_wq_ref[...] = dot3(lat_ref[...], both[:, :DH], 0, 0)
    d_wo_ref[...] = dot3(both[:, DH:], dout_ref[...], 0, 0)


def on_device(latents, observations, w_query, w_key, w_value, w_out, d_out):
    scale = 1.0 / math.sqrt(DH)
    lat = latents.shape[0]
    width = observations.shape[1]
    n_ctx, n_head = lax.axis_size("ctx"), lax.axis_size("head")
    nz, nx = n_ctx // NY, n_head // 2
    ctx, head = lax.axis_index("ctx"), lax.axis_index("head")
    z, y = ctx // NY, ctx % NY
    x, core = head // 2, head % 2
    z_groups = [[a * NY + b for a in range(nz)] for b in range(NY)]
    swap = [(i, i ^ 1) for i in range(n_head)]
    right = [(i, (i + 2) % n_head) for i in range(n_head)]
    left = [(i, (i - 2) % n_head) for i in range(n_head)]
    rows_y = lat // NY
    rows_z = rows_y // nz

    def along_y(k):
        return [(i, i - i % NY + (i + k) % NY) for i in range(n_ctx)]

    kv, q3, g3, sent, stat, given = forward(
        n_ctx, core.reshape(1), latents, d_out, w_query, w_out, w_key, w_value, observations
    )
    stats = lax.all_to_all(sent, "ctx", 0, 0)
    taken = lax.ppermute(given, "head", swap)
    parts = local_sums(y.reshape(1), kv, q3, g3, stat)
    parts = [parts[0]] + [lax.ppermute(parts[k], "ctx", along_y(k)) for k in range(1, NY)]
    (w_chip,) = small_call(
        chip_weights_kernel, [shape(nx, 2 * DH, 4 * DH, dtype=BF16)],
        [w_key, w_value, taken], [jnp.stack([x, core])], after=[parts[0]], name="chip_weights",
    )
    stat, shares, deltas = small_call(
        combine_kernel,
        [shape(3, lat), shape(n_ctx, 1, lat), shape(n_ctx, 1, lat)],
        [stats], [], after=[w_chip], name="combine",
    )

    def half_grads(h):
        own = token_grads(h, kv, q3, g3, stat)
        return own, lax.ppermute(own, "head", swap)

    a, b = half_grads(0), half_grads(1)
    half = a[0].shape[0]
    right_1, left_1 = token_part(
        first_kernel, a, b, w_chip, (2, 1, 3), b[0], (), [shape(2, half, DH)] * 2, "token_first"
    )
    from_left_1 = lax.ppermute(right_1, "head", right)
    from_right_1 = lax.ppermute(left_1, "head", left)

    (both,) = small_call(
        lambda *refs: rows_kernel(scale, *refs), [shape(rows_y, 2 * DH)],
        [shares, deltas, *parts], [jnp.stack([z, y])], after=[right_1], name="rows",
    )
    rows = lax.all_to_all(
        both.reshape(nz, rows_z, 2 * DH), "ctx", 0, 0, axis_index_groups=z_groups
    )
    d_w = weight_grads(both, y.reshape(1), nz, observations, a[0], b[0])
    d_w = [d_w[0]] + [lax.ppermute(d_w[k], "ctx", along_y(k)) for k in range(1, NY)]
    rows, part = small_call(
        latent_part_kernel, [shape(rows_z, 2 * DH), shape(n_head, rows_z, DH)],
        [rows, w_query], [], after=[d_w[0]], name="latent_part",
    )
    part = lax.all_to_all(part, "head", 0, 0)
    (sent,) = small_call(
        latent_rows_kernel, [shape(nz, rows_z, 7 * DH)], [rows, part, *d_w], [],
        name="latent_rows",
    )
    got = lax.all_to_all(sent, "ctx", 0, 0, axis_index_groups=z_groups)
    right_2, left_2 = token_part(
        second_kernel, a, b, w_chip, (1, 3), sent, (from_left_1, from_right_1),
        [shape(half, DH)] * 2, "token_second",
    )
    from_left_2 = lax.ppermute(right_2, "head", right)
    from_right_2 = lax.ppermute(left_2, "head", left)
    rows, d_w_key, d_w_value = small_call(
        gathered_kernel,
        [shape(rows_y, 3 * DH), shape(width // n_ctx, DH), shape(width // n_ctx, DH)],
        [got], [], after=[right_2], name="gathered",
    )
    rows = [rows] + [lax.ppermute(rows, "ctx", along_y(k)) for k in range(1, NY)]
    d_latents, d_w_query, d_w_out = small_call(
        final_kernel, [shape(lat, DH), shape(width, DH), shape(DH, width)],
        [*rows, latents, d_out], [y.reshape(1)], scratch=[VMEM((lat, 2 * DH), F32)], name="final",
    )
    d_observations = token_last(a, b, w_chip, from_left_1, from_right_1, from_left_2, from_right_2)
    return (d_latents, d_observations, d_w_query, d_w_key, d_w_value, d_w_out)


def solution(mesh):
    placed = (
        P(),
        P("ctx", None),
        P(None, "head"),
        P(None, "head"),
        P(None, "head"),
        P("head", None),
        P(),
    )
    return jax.shard_map(
        on_device,
        mesh=mesh,
        in_specs=placed,
        out_specs=(
            P(None, "head"),
            P("ctx", "head"),
            P(None, "head"),
            P("ctx", "head"),
            P("ctx", "head"),
            P("head", None),
        ),
        check_vma=False,
    )
```

time: 539 us -> 153 us (0.28)
  waiting for transfers between devices: 306 us -> 21.7 us
  blocking collectives: 121 us -> 0 us
  matrix products: 86.5 us -> 0 us
  Pallas kernels: 0 us -> 51.3 us
  starting transfers between devices: 0.38 us -> 50.7 us
  local copies, waits for them, and re-layouts: 4.33 us -> 26.7 us
  between operations: 14.3 us -> 0.86 us
    psum x2 -> x0, waiting for transfers between devices: 238 us -> none  [the longest x1 148 us: on_device(): dquery = lax.psum(dquery_part, 'ctx')]
    dot_general x16 -> x0, matrix products: 86.5 us -> none  [the longest x1 10.2 us: on_device(): jnp.dot(observations, w_key, precision=highest, preferred_element_type=jn...]
    reduce_scatter x2 -> x0, waiting for transfers between devices: 67.8 us -> none  [the longest x1 59.1 us: on_device(): lax.psum_scatter(token_part, 'head', scatter_dimension=1, tiled=True)]
    pmax x1 -> x0, blocking collectives: 64.9 us -> none  [on_device(): top = lax.pmax(row_max, 'ctx')]
    psum x1 -> x0, blocking collectives: 56.1 us -> none  [on_device(): lax.psum((jnp.sum(expo, axis=2), jnp.einsum('hlt,thd->hld', expo, values_...]
    pallas_call x0 -> x15, Pallas kernels: none -> 51.3 us  [the longest x1 14.2 us: forward(): pl.pallas_call(lambda *refs: forward_kernel(1.0 / math.sqrt(DH), *refs),...]
    all_to_all x0 -> x4, starting transfers between devices: none -> 29.7 us  [the longest x1 9.47 us: on_device(): stats = lax.all_to_all(sent, 'ctx', 0, 0)]
    unnamed x33 -> x62, local copies, waits for them, and re-layouts: 3.37 us -> 26.7 us
  transfers between devices with their start and end apart: 4 -> 20, of which waited for: 4 -> 6; matrix products, arithmetic and copies ran while one was open for 5% -> 0% of each run, Pallas kernels for 0% -> 18%
where the time goes in v1:
time: 153 us; the launch traced here: 151 us
  Pallas kernels  51.3 us (34%)
  starting transfers between devices  50.7 us (33%)
  local copies, waits for them, and re-layouts  26.7 us (17%)
  waiting for transfers between devices  21.7 us (14%)
    unnamed x62, local copies, waits for them, and re-layouts  26.7 us
    pallas_call x1, Pallas kernels, forward(): pl.pallas_call(lambda *refs: forward_kernel(1.0 / math.sqrt(DH), *refs),...  14.2 us
    all_to_all x1, starting transfers between devices, on_device(): stats = lax.all_to_all(sent, 'ctx', 0, 0)  9.47 us
    ppermute x3, waiting for transfers between devices, on_device(): lax.ppermute(rows, 'ctx', along_y(k))  8.59 us
    pallas_call x7, Pallas kernels, small_call(): pl.pallas_call(body, in_specs=[ANY] * len(after) + [SCALARS] * len(scalar...  7.73 us
    all_to_all x1, starting transfers between devices, on_device(): part = lax.all_to_all(part, 'head', 0, 0)  6.93 us
    all_to_all x1, starting transfers between devices, on_device(): got = lax.all_to_all(sent, 'ctx', 0, 0, axis_index_groups=z_groups)  6.93 us
    pallas_call x1, Pallas kernels, local_sums(): pl.pallas_call(sums_kernel, grid=(tok // CHUNK,), in_specs=[SCALARS, bloc...  6.82 us
  transfers between devices with their start and end apart: 20, of which 6 were waited for; matrix products, arithmetic and copies ran while one was open for 0% of the time, Pallas kernels for 18%

profile of v1, /device:TPU:1, one launch (start us, length us, event | category | flops | bytes accessed | tf_op | source)
XLA Modules:
  0.0 151.4 jit_solution(3924890693956375902)
XLA Ops:
  0.6 14.2 %forward.1 = (bf16[2048,512]{1,0:T(8,128)(2,1)}, bf16[512,384]{1,0:T(8,128)(2,1)}, bf16[512,384]{1,0:T(8,128)(2,1)}, f32[32,3,512]{2,1,0:T(4,128)}, f32[3,512]{1,0:T(4,128)}, /*index=5*/f32[4,128,256]{2,1,0:T(8,128)}) custom-call(s32[1]{0:T(128)} %bitcast.1.refs_0_, f32[512,1024]{1,0:T(8,128)} %refs_5_.3, f32[512,1024]{1,0:T(8,128)} %refs_6_.3, ...), custom_call_target="tpu_custom_call" | custom-call | flops 4831838208 | bytes 18874368 | tf_op jit(solution)/shard_map/forward/pallas_call | solution.py:141
  14.8 3.3 %collective-permute-start = (f32[4,128,256]{2,1,0:T(8,128)}, f32[4,128,256]{2,1,0:T(8,128)S(1)}, u32[]{:S(2)}, u32[]{:S(2)}) collective-permute-start(f32[4,128,256]{2,1,0:T(8,128)} %get-tuple-element.40), channel_id=1, source_target_pairs={{0,1},{1,0},{2,3},{3,2},{4,5},{5,4},{6,7},{7,6},{8,9},{9,8},{10,11... | collective-permute-start | bytes 1572872 | tf_op jit(solution)/shard_map/ppermute | solution.py:490
  18.2 9.5 %all-to-all-start = ((f32[32,3,512]{2,1,0:T(4,128)}), f32[32,3,512]{2,1,0:T(4,128)S(1)}, u32[]{:S(2)}, u32[]{:S(2)}) async-start(f32[32,3,512]{2,1,0:T(4,128)} %get-tuple-element.41), calls=%async_computation | async-start | bytes 524288 | tf_op jit(solution)/shard_map/all_to_all | solution.py:489
  32.0 6.8 %local_sums.1 = (f32[128,384]{1,0:T(8,128)S(1)}, f32[128,384]{1,0:T(8,128)}, f32[128,384]{1,0:T(8,128)}, f32[128,384]{1,0:T(8,128)}) custom-call(s32[1]{0:T(128)} %bitcast.y_ref.refs_0_, bf16[2048,512]{1,0:T(8,128)(2,1)S(1)} %copy-done.23, bf16[512,384]{1,0:T(8,128)(2,1)S(1)} %copy-done.25, bf16[512,384]{1,0:T(8,128)(2,1)S(1)} %copy-done.28, ...), custom_call_target="tpu_custom_call" | custom-call | flops 2415919104 | bytes 12582912 | tf_op jit(solution)/shard_map/local_sums/pallas_call | solution.py:203
  46.4 2.7 %token_grads.3.refs_1_.a_ref.own_a = f32[1024,256]{1,0:T(8,128)S(1)} custom-call(bf16[2048,512]{1,0:T(8,128)(2,1)S(1)} %copy-done.24, bf16[512,384]{1,0:T(8,128)(2,1)S(1)} %copy-done.26, bf16[512,384]{1,0:T(8,128)(2,1)S(1)} %copy-done.29, f32[3,512]{1,0:T(4,128)S(1)} %get-tuple-element.42.stat_ref), custom_call_target="tpu_custom_call" | custom-call | flops 1610612736 | bytes 5242880 | tf_op jit(solution)/shard_map/token_grads/pallas_call | solution.py:231
  49.1 2.7 %token_grads.2.refs_0_.refs_3_.b_ref.own_b = f32[1024,256]{1,0:T(8,128)S(1)} custom-call(bf16[2048,512]{1,0:T(8,128)(2,1)S(1)} %copy-done.24, bf16[512,384]{1,0:T(8,128)(2,1)S(1)} %copy-done.27, bf16[512,384]{1,0:T(8,128)(2,1)S(1)} %copy-done.29, f32[3,512]{1,0:T(4,128)S(1)} %get-tuple-element.42.stat_ref), custom_call_target="tpu_custom_call" | custom-call | flops 1610612736 | bytes 5242880 | tf_op jit(solution)/shard_map/token_grads/pallas_call | solution.py:231
  53.8 2.4 %collective-permute-start.4 = (f32[128,384]{1,0:T(8,128)}, f32[128,384]{1,0:T(8,128)}, u32[]{:S(2)}, u32[]{:S(2)}) collective-permute-start(f32[128,384]{1,0:T(8,128)} %get-tuple-element.47), channel_id=1, source_target_pairs={{0,16},{8,24},{16,0},{24,8},{32,48},{40,56},{48,32},{56,40},{64,80... | collective-permute-start | bytes 589832 | tf_op jit(solution)/shard_map/ppermute | solution.py:492
  57.4 3.6 %token_first.1 = (f32[2,1024,128]{2,1,0:T(8,128)}, f32[2,1024,128]{2,1,0:T(8,128)}) custom-call(f32[1024,256]{1,0:T(8,128)S(1)} %token_grads.2.refs_0_.refs_3_.b_ref.own_b, f32[1024,256]{1,0:T(8,128)S(1)} %token_grads.3.refs_1_.a_ref.own_a, f32[1024,256]{1,0:T(8,128)S(1)} %collective-permute-done.1.refs_2_.other_a, ...), custom_call_target="tpu_custom_call" | custom-call | flops 1610612736 | bytes 6291456 | tf_op jit(solution)/shard_map/token_first/pallas_call | solution.py:274
  61.1 2.5 %collective-permute-start.10 = (f32[2,1024,128]{2,1,0:T(8,128)}, f32[2,1024,128]{2,1,0:T(8,128)}, u32[]{:S(2)}, u32[]{:S(2)}) collective-permute-start(f32[2,1024,128]{2,1,0:T(8,128)} %get-tuple-element.55), channel_id=1, source_target_pairs={{0,6},{1,7},{2,0},{3,1},{4,2},{5,3},{6,4},{7,5},{8,14},{9,15},{10,... | collective-permute-start | bytes 3145736 | tf_op jit(solution)/shard_map/ppermute | solution.py:513
  63.6 1.8 %collective-permute-done.4.refs_6_ = f32[128,384]{1,0:T(8,128)} collective-permute-done((f32[128,384]{1,0:T(8,128)}, f32[128,384]{1,0:T(8,128)}, u32[]{:S(2)}, u32[]{:S(2)}) %collective-permute-start.4) | collective-permute-done | bytes 196640 | tf_op jit(solution)/shard_map/ppermute | solution.py:492
  68.9 6.4 %all-to-all-start.1 = ((f32[8,16,256]{2,1,0:T(8,128)}), f32[8,16,256]{2,1,0:T(8,128)S(1)}, u32[]{:S(2)}, u32[]{:S(2)}) async-start(f32[8,16,256]{2,1,0:T(8,128)} %bitcast.5), calls=%async_computation.1 | async-start | bytes 262144 | tf_op jit(solution)/shard_map/all_to_all | solution.py:519
  76.3 3.4 %copy-done.22 = f32[2048,1024]{1,0:T(8,128)S(1)} copy-done((f32[2048,1024]{1,0:T(8,128)S(1)}, f32[2048,1024]{1,0:T(8,128)}, u32[]{:S(2)}) %copy-start.22) | copy-done | bytes 8388632
  79.6 5.8 %weight_grads.1 = (f32[8,32,256]{2,1,0:T(8,128)S(1)}, f32[8,32,256]{2,1,0:T(8,128)}, f32[8,32,256]{2,1,0:T(8,128)}, f32[8,32,256]{2,1,0:T(8,128)}) custom-call(f32[128,256]{1,0:T(8,128)S(1)} %copy-done.12, s32[1]{0:T(128)} %bitcast.y_ref.refs_0_, f32[2048,1024]{1,0:T(8,128)S(1)} %copy-done.22, f32[1024,256]{1,0:T(8,128)S(1)} %token_grads.3.refs_1_.a_ref.own_a, ...), custom_call_target="tpu_custom_call" | custom-call | flops 3221225472 | bytes 11534336 | tf_op jit(solution)/shard_map/weight_grads/pallas_call | solution.py:353
  86.6 2.8 %collective-permute-start.7 = (f32[8,32,256]{2,1,0:T(8,128)}, f32[8,32,256]{2,1,0:T(8,128)}, u32[]{:S(2)}, u32[]{:S(2)}) collective-permute-start(f32[8,32,256]{2,1,0:T(8,128)} %get-tuple-element.53), channel_id=1, source_target_pairs={{0,16},{8,24},{16,0},{24,8},{32,48},{40,56},{48,32},{56,40},{64,80... | collective-permute-start | bytes 786440 | tf_op jit(solution)/shard_map/ppermute | solution.py:523
  91.6 6.9 %all-to-all-start.2 = ((f32[8,16,128]{2,1,0:T(8,128)}), f32[8,16,128]{2,1,0:T(8,128)S(1)}, u32[]{:S(2)}, u32[]{:S(2)}) async-start(f32[8,16,128]{2,1,0:T(8,128)} %copy-done.21), calls=%async_computation.2 | async-start | bytes 131072 | tf_op jit(solution)/shard_map/all_to_all | solution.py:528
  98.5 2.4 %collective-permute-done.7.refs_4_ = f32[8,32,256]{2,1,0:T(8,128)} collective-permute-done((f32[8,32,256]{2,1,0:T(8,128)}, f32[8,32,256]{2,1,0:T(8,128)}, u32[]{:S(2)}, u32[]{:S(2)}) %collective-permute-start.7) | collective-permute-done | bytes 262176 | tf_op jit(solution)/shard_map/ppermute | solution.py:523
  100.9 2.4 %all-to-all-done.2.refs_1_ = f32[8,16,128]{2,1,0:T(8,128)S(1)} async-done(((f32[8,16,128]{2,1,0:T(8,128)}), f32[8,16,128]{2,1,0:T(8,128)S(1)}, u32[]{:S(2)}, u32[]{:S(2)}) %all-to-all-start.2) | async-done | bytes 65568 | tf_op jit(solution)/shard_map/all_to_all | solution.py:528
  105.3 6.9 %all-to-all-start.3 = ((f32[8,16,896]{2,1,0:T(8,128)}), f32[8,16,896]{2,1,0:T(8,128)}, u32[]{:S(2)}, u32[]{:S(2)}) async-start(f32[8,16,896]{2,1,0:T(8,128)} %copy-done.6), calls=%async_computation.3 | async-start | bytes 917504 | tf_op jit(solution)/shard_map/all_to_all | solution.py:533
  115.7 3.2 %token_second.1 = (f32[1024,128]{1,0:T(8,128)}, f32[1024,128]{1,0:T(8,128)}) custom-call(f32[8,16,896]{2,1,0:T(8,128)S(1)} %copy-done.7, f32[1024,256]{1,0:T(8,128)S(1)} %token_grads.3.refs_1_.a_ref.own_a, f32[1024,256]{1,0:T(8,128)S(1)} %copy-done.1, f32[1024,256]{1,0:T(8,128)S(1)} %token_grads.2.refs_0_.refs_3_.b_ref.own_b, f32[1024,256]{1,0:T(8,128)S(1)} %copy-done.4, ...), custom_call_target="tpu_custom_call" | custom-call | flops 1610612736 | bytes 6291456 | tf_op jit(solution)/shard_map/token_second/pallas_call | solution.py:274
  119.2 2.4 %collective-permute-start.15 = (f32[1024,128]{1,0:T(8,128)}, f32[1024,128]{1,0:T(8,128)}, u32[]{:S(2)}, u32[]{:S(2)}) collective-permute-start(f32[1024,128]{1,0:T(8,128)} %get-tuple-element.59), channel_id=1, source_target_pairs={{0,6},{1,7},{2,0},{3,1},{4,2},{5,3},{6,4},{7,5},{8,14},{9,15},{10,... | collective-permute-start | bytes 1572872 | tf_op jit(solution)/shard_map/ppermute | solution.py:539
  121.6 6.5 %all-to-all-done.3.refs_1_ = f32[8,16,896]{2,1,0:T(8,128)} async-done(((f32[8,16,896]{2,1,0:T(8,128)}), f32[8,16,896]{2,1,0:T(8,128)}, u32[]{:S(2)}, u32[]{:S(2)}) %all-to-all-start.3) | async-done | bytes 458784 | tf_op jit(solution)/shard_map/all_to_all | solution.py:533
  132.5 8.3 %collective-permute-done.11.refs_2_ = f32[128,384]{1,0:T(8,128)S(1)} collective-permute-done((f32[128,384]{1,0:T(8,128)S(1)}, f32[128,384]{1,0:T(8,128)S(1)}, u32[]{:S(2)}, u32[]{:S(2)}) %collective-permute-start.11) | collective-permute-done | bytes 196640 | tf_op jit(solution)/shard_map/ppermute | solution.py:545
  144.2 2.5 %final.1 = (f32[512,128]{1,0:T(8,128)}, f32[1024,128]{1,0:T(8,128)}, f32[128,1024]{1,0:T(8,128)}) custom-call(s32[1]{0:T(128)} %bitcast.y_ref.refs_0_, f32[128,384]{1,0:T(8,128)S(1)} %get-tuple-element.57.refs_1_, f32[128,384]{1,0:T(8,128)S(1)} %collective-permute-done.11.refs_2_, f32[128,384]{1,0:T(8,128)S(1)} %collective-permute-done.12.refs_3_, ...), custom_call_target="tpu_custom_call" | custom-call | flops 6291456 | bytes 1048576 | tf_op jit(solution)/shard_map/final/pallas_call | solution.py:375
  146.8 4.6 %token_last.1 = f32[2048,128]{1,0:T(8,128)} custom-call(f32[1024,256]{1,0:T(8,128)S(1)} %token_grads.3.refs_1_.a_ref.own_a, f32[1024,256]{1,0:T(8,128)S(1)} %copy-done.2, f32[1024,256]{1,0:T(8,128)S(1)} %token_grads.2.refs_0_.refs_3_.b_ref.own_b, f32[1024,256]{1,0:T(8,128)S(1)} %copy-done.5, ...), custom_call_target="tpu_custom_call" | custom-call | flops 805306368 | bytes 8388608 | tf_op jit(solution)/shard_map/token_last/pallas_call | solution.py:306
  (95 shorter events, 36.6 us)
Async XLA Ops:
  14.8 24.0 %collective-permute-start = (f32[4,128,256]{2,1,0:T(8,128)}, f32[4,128,256]{2,1,0:T(8,128)S(1)}, u32[]{:S(2)}, u32[]{:S(2)}) collective-permute-start(f32[4,128,256]{2,1,0:T(8,128)} %get-tuple-element.40), channel_id=1, source_target_pairs={{0,1},{1,0},{2,3},{3,2},{4,5},{5,4},{6,7},{7,6},{8,9},{9,8},{10,11... | collective-permute-start | bytes 1572872 | tf_op jit(solution)/shard_map/ppermute | solution.py:490
  18.2 23.3 %all-to-all-start = ((f32[32,3,512]{2,1,0:T(4,128)}), f32[32,3,512]{2,1,0:T(4,128)S(1)}, u32[]{:S(2)}, u32[]{:S(2)}) async-start(f32[32,3,512]{2,1,0:T(4,128)} %get-tuple-element.41), calls=%async_computation | async-start | bytes 524288 | tf_op jit(solution)/shard_map/all_to_all | solution.py:489
  32.0 7.6 %copy-start.13 = (f32[1024,128]{1,0:T(8,128)S(1)}, f32[1024,128]{1,0:T(8,128)}, u32[]{:S(2)}) copy-start(f32[1024,128]{1,0:T(8,128)} %refs_2_.4) | copy-start | bytes 1572868
  32.0 7.6 %copy-start.14 = (f32[1024,128]{1,0:T(8,128)S(1)}, f32[1024,128]{1,0:T(8,128)}, u32[]{:S(2)}) copy-start(f32[1024,128]{1,0:T(8,128)} %refs_3_.3) | copy-start | bytes 1572868
  51.8 5.6 %collective-permute-start.1 = (f32[1024,256]{1,0:T(8,128)S(1)}, f32[1024,256]{1,0:T(8,128)S(1)}, u32[]{:S(2)}, u32[]{:S(2)}) collective-permute-start(f32[1024,256]{1,0:T(8,128)S(1)} %token_grads.3.refs_1_.a_ref.own_a), channel_id=1, source_target_pairs={{0,1},{1,0},{2,3},{3,2},{4,5},{5,4},{6,7},{7,6},{8,9},{9,8},{10,11... | collective-permute-start | bytes 3145736 | tf_op jit(solution)/shard_map/ppermute | solution.py:505
  52.2 5.2 %collective-permute-start.2 = (f32[1024,256]{1,0:T(8,128)S(1)}, f32[1024,256]{1,0:T(8,128)S(1)}, u32[]{:S(2)}, u32[]{:S(2)}) collective-permute-start(f32[1024,256]{1,0:T(8,128)S(1)} %token_grads.2.refs_0_.refs_3_.b_ref.own_b), channel_id=1, source_target_pairs={{0,1},{1,0},{2,3},{3,2},{4,5},{5,4},{6,7},{7,6},{8,9},{9,8},{10,11... | collective-permute-start | bytes 3145736 | tf_op jit(solution)/shard_map/ppermute | solution.py:505
  52.4 11.2 %collective-permute-start.3 = (f32[128,384]{1,0:T(8,128)}, f32[128,384]{1,0:T(8,128)S(1)}, u32[]{:S(2)}, u32[]{:S(2)}) collective-permute-start(f32[128,384]{1,0:T(8,128)} %get-tuple-element.46), channel_id=1, source_target_pairs={{0,8},{8,16},{16,24},{24,0},{32,40},{40,48},{48,56},{56,32},{64,72... | collective-permute-start | bytes 589832 | tf_op jit(solution)/shard_map/ppermute | solution.py:492
  53.8 11.5 %collective-permute-start.4 = (f32[128,384]{1,0:T(8,128)}, f32[128,384]{1,0:T(8,128)}, u32[]{:S(2)}, u32[]{:S(2)}) collective-permute-start(f32[128,384]{1,0:T(8,128)} %get-tuple-element.47), channel_id=1, source_target_pairs={{0,16},{8,24},{16,0},{24,8},{32,48},{40,56},{48,32},{56,40},{64,80... | collective-permute-start | bytes 589832 | tf_op jit(solution)/shard_map/ppermute | solution.py:492
  56.2 9.1 %collective-permute-start.5 = (f32[128,384]{1,0:T(8,128)}, f32[128,384]{1,0:T(8,128)}, u32[]{:S(2)}, u32[]{:S(2)}) collective-permute-start(f32[128,384]{1,0:T(8,128)} %get-tuple-element.48), channel_id=1, source_target_pairs={{0,24},{8,0},{16,8},{24,16},{32,56},{40,32},{48,40},{56,48},{64,88... | collective-permute-start | bytes 589832 | tf_op jit(solution)/shard_map/ppermute | solution.py:492
  61.1 51.2 %collective-permute-start.10 = (f32[2,1024,128]{2,1,0:T(8,128)}, f32[2,1024,128]{2,1,0:T(8,128)}, u32[]{:S(2)}, u32[]{:S(2)}) collective-permute-start(f32[2,1024,128]{2,1,0:T(8,128)} %get-tuple-element.55), channel_id=1, source_target_pairs={{0,6},{1,7},{2,0},{3,1},{4,2},{5,3},{6,4},{7,5},{8,14},{9,15},{10,... | collective-permute-start | bytes 3145736 | tf_op jit(solution)/shard_map/ppermute | solution.py:513
  63.5 48.7 %collective-permute-start.9 = (f32[2,1024,128]{2,1,0:T(8,128)}, f32[2,1024,128]{2,1,0:T(8,128)}, u32[]{:S(2)}, u32[]{:S(2)}) collective-permute-start(f32[2,1024,128]{2,1,0:T(8,128)} %get-tuple-element.43.refs_0_), channel_id=1, source_target_pairs={{0,2},{1,3},{2,4},{3,5},{4,6},{5,7},{6,0},{7,1},{8,10},{9,11},{10,... | collective-permute-start | bytes 3145736 | tf_op jit(solution)/shard_map/ppermute | solution.py:512
  68.9 20.7 %all-to-all-start.1 = ((f32[8,16,256]{2,1,0:T(8,128)}), f32[8,16,256]{2,1,0:T(8,128)S(1)}, u32[]{:S(2)}, u32[]{:S(2)}) async-start(f32[8,16,256]{2,1,0:T(8,128)} %bitcast.5), calls=%async_computation.1 | async-start | bytes 262144 | tf_op jit(solution)/shard_map/all_to_all | solution.py:519
  85.4 13.1 %collective-permute-start.6 = (f32[8,32,256]{2,1,0:T(8,128)}, f32[8,32,256]{2,1,0:T(8,128)}, u32[]{:S(2)}, u32[]{:S(2)}) collective-permute-start(f32[8,32,256]{2,1,0:T(8,128)} %get-tuple-element.52), channel_id=1, source_target_pairs={{0,8},{8,16},{16,24},{24,0},{32,40},{40,48},{48,56},{56,32},{64,72... | collective-permute-start | bytes 786440 | tf_op jit(solution)/shard_map/ppermute | solution.py:523
  86.6 14.3 %collective-permute-start.7 = (f32[8,32,256]{2,1,0:T(8,128)}, f32[8,32,256]{2,1,0:T(8,128)}, u32[]{:S(2)}, u32[]{:S(2)}) collective-permute-start(f32[8,32,256]{2,1,0:T(8,128)} %get-tuple-element.53), channel_id=1, source_target_pairs={{0,16},{8,24},{16,0},{24,8},{32,48},{40,56},{48,32},{56,40},{64,80... | collective-permute-start | bytes 786440 | tf_op jit(solution)/shard_map/ppermute | solution.py:523
  89.4 11.5 %collective-permute-start.8 = (f32[8,32,256]{2,1,0:T(8,128)}, f32[8,32,256]{2,1,0:T(8,128)}, u32[]{:S(2)}, u32[]{:S(2)}) collective-permute-start(f32[8,32,256]{2,1,0:T(8,128)} %get-tuple-element.54), channel_id=1, source_target_pairs={{0,24},{8,0},{16,8},{24,16},{32,56},{40,32},{48,40},{56,48},{64,88... | collective-permute-start | bytes 786440 | tf_op jit(solution)/shard_map/ppermute | solution.py:523
  91.6 11.8 %all-to-all-start.2 = ((f32[8,16,128]{2,1,0:T(8,128)}), f32[8,16,128]{2,1,0:T(8,128)S(1)}, u32[]{:S(2)}, u32[]{:S(2)}) async-start(f32[8,16,128]{2,1,0:T(8,128)} %copy-done.21), calls=%async_computation.2 | async-start | bytes 131072 | tf_op jit(solution)/shard_map/all_to_all | solution.py:528
  105.3 22.8 %all-to-all-start.3 = ((f32[8,16,896]{2,1,0:T(8,128)}), f32[8,16,896]{2,1,0:T(8,128)}, u32[]{:S(2)}, u32[]{:S(2)}) async-start(f32[8,16,896]{2,1,0:T(8,128)} %copy-done.6), calls=%async_computation.3 | async-start | bytes 917504 | tf_op jit(solution)/shard_map/all_to_all | solution.py:533
  118.9 27.8 %collective-permute-start.14 = (f32[1024,128]{1,0:T(8,128)}, f32[1024,128]{1,0:T(8,128)}, u32[]{:S(2)}, u32[]{:S(2)}) collective-permute-start(f32[1024,128]{1,0:T(8,128)} %get-tuple-element.56.refs_0_), channel_id=1, source_target_pairs={{0,2},{1,3},{2,4},{3,5},{4,6},{5,7},{6,0},{7,1},{8,10},{9,11},{10,... | collective-permute-start | bytes 1572872 | tf_op jit(solution)/shard_map/ppermute | solution.py:538
  119.2 27.5 %collective-permute-start.15 = (f32[1024,128]{1,0:T(8,128)}, f32[1024,128]{1,0:T(8,128)}, u32[]{:S(2)}, u32[]{:S(2)}) collective-permute-start(f32[1024,128]{1,0:T(8,128)} %get-tuple-element.59), channel_id=1, source_target_pairs={{0,6},{1,7},{2,0},{3,1},{4,2},{5,3},{6,4},{7,5},{8,14},{9,15},{10,... | collective-permute-start | bytes 1572872 | tf_op jit(solution)/shard_map/ppermute | solution.py:539
  129.7 17.0 %copy-start.2 = (f32[1024,256]{1,0:T(8,128)S(1)}, f32[1024,256]{1,0:T(8,128)}, u32[]{:S(2)}) copy-start(f32[1024,256]{1,0:T(8,128)} %copy-done) | copy-start | bytes 3145732
  129.7 17.0 %copy-start.5 = (f32[1024,256]{1,0:T(8,128)S(1)}, f32[1024,256]{1,0:T(8,128)}, u32[]{:S(2)}) copy-start(f32[1024,256]{1,0:T(8,128)} %copy-done.3) | copy-start | bytes 3145732
  129.7 11.0 %collective-permute-start.11 = (f32[128,384]{1,0:T(8,128)S(1)}, f32[128,384]{1,0:T(8,128)S(1)}, u32[]{:S(2)}, u32[]{:S(2)}) collective-permute-start(f32[128,384]{1,0:T(8,128)S(1)} %get-tuple-element.57.refs_1_), channel_id=1, source_target_pairs={{0,8},{8,16},{16,24},{24,0},{32,40},{40,48},{48,56},{56,32},{64,72... | collective-permute-start | bytes 589832 | tf_op jit(solution)/shard_map/ppermute | solution.py:545
  130.0 10.8 %collective-permute-start.12 = (f32[128,384]{1,0:T(8,128)S(1)}, f32[128,384]{1,0:T(8,128)S(1)}, u32[]{:S(2)}, u32[]{:S(2)}) collective-permute-start(f32[128,384]{1,0:T(8,128)S(1)} %get-tuple-element.57.refs_1_), channel_id=1, source_target_pairs={{0,16},{8,24},{16,0},{24,8},{32,48},{40,56},{48,32},{56,40},{64,80... | collective-permute-start | bytes 589832 | tf_op jit(solution)/shard_map/ppermute | solution.py:545
  130.8 10.3 %collective-permute-start.13 = (f32[128,384]{1,0:T(8,128)S(1)}, f32[128,384]{1,0:T(8,128)S(1)}, u32[]{:S(2)}, u32[]{:S(2)}) collective-permute-start(f32[128,384]{1,0:T(8,128)S(1)} %get-tuple-element.57.refs_1_), channel_id=1, source_target_pairs={{0,24},{8,0},{16,8},{24,16},{32,56},{40,32},{48,40},{56,48},{64,88... | collective-permute-start | bytes 589832 | tf_op jit(solution)/shard_map/ppermute | solution.py:545
  (27 other events, 36.6 us)

commit v2 on v1

v2 whole, which is shorter than its diff:
```python
import math

import jax
import jax.numpy as jnp
from jax import lax
from jax.experimental import pallas as pl
from jax.experimental.pallas import tpu as pltpu
from jax.sharding import PartitionSpec as P

DH = 128
NY = 4
CHUNK = 512
F32 = jnp.float32
BF16 = jnp.bfloat16
VMEM = pltpu.VMEM
WHOLE = pl.BlockSpec(memory_space=VMEM)
ANY = pl.BlockSpec(memory_space=pl.ANY)
HBM = pl.BlockSpec(memory_space=pltpu.HBM)
SCALARS = pl.BlockSpec(memory_space=pltpu.SMEM)


def shape(*dims, dtype=F32):
    return jax.ShapeDtypeStruct(dims, dtype)


def pin(a, space):
    return pltpu.with_memory_space_constraint(a, space)


def params(mib):
    return pltpu.CompilerParams(vmem_limit_bytes=mib << 20)


def cost(macs, bytes_accessed):
    return pl.CostEstimate(flops=6 * macs, bytes_accessed=bytes_accessed, transcendentals=0)


def mm(a, b, ca=1, cb=0):
    return lax.dot_general(a, b, (((ca,), (cb,)), ((), ())), preferred_element_type=F32)


def split(a):
    hi = a.astype(BF16)
    return hi, (a - hi.astype(F32)).astype(BF16)


def dot3(a, b, ca=1, cb=0):
    a_hi, a_lo = split(a)
    b_hi, b_lo = split(b)
    return mm(a_hi, b_hi, ca, cb) + mm(a_hi, b_lo, ca, cb) + mm(a_lo, b_hi, ca, cb)


def scores_of(kv_ref, q3, g3):
    hi_k, hi_v, lo_k, lo_v = (kv_ref[:, i * DH : (i + 1) * DH] for i in range(4))
    scores = mm(jnp.concatenate([hi_k, lo_k, hi_k], axis=1), q3[...], 1, 1)
    return scores, mm(jnp.concatenate([hi_v, lo_v, hi_v], axis=1), g3[...], 1, 1)


def forward_kernel(
    scale, core_ref, lat_hbm, dout_hbm, wq_hbm, wo_hbm, wk_hbm, wv_hbm, obs_hbm,
    kv_ref, q3, g3, sent_ref, stat_ref, given_ref,
    lat_v, dout_v, wq_v, wo_v, wk_v, wv_v, obs_v, sems, obs_sems, w_hi, w_lo,
):
    step = pl.program_id(0)
    loads = [
        pltpu.make_async_copy(source, target, sems.at[i])
        for i, (source, target) in enumerate(
            (
                (wk_hbm, wk_v), (wv_hbm, wv_v), (lat_hbm, lat_v),
                (wq_hbm, wq_v), (dout_hbm, dout_v), (wo_hbm, wo_v),
            )
        )
    ]

    def load_tokens(i):
        rows = pl.ds(pl.multiple_of(i * CHUNK, CHUNK), CHUNK)
        return pltpu.make_async_copy(obs_hbm.at[rows], obs_v.at[i], obs_sems.at[i])

    @pl.when(step == 0)
    def _():
        loads[0].start()
        loads[1].start()
        load_tokens(0).start()
        for load in loads[2:]:
            load.start()
        for i in range(1, obs_v.shape[0]):
            load_tokens(i).start()
        loads[0].wait()
        loads[1].wait()
        hi, lo = split(wk_v[...])
        w_hi[:, :DH], w_lo[:, :DH] = hi, lo
        hi, lo = split(wv_v[...])
        w_hi[:, DH:], w_lo[:, DH:] = hi, lo
        for d in range(given_ref.shape[0]):
            at = pl.ds(pl.multiple_of((2 * d + 1 - core_ref[0]) * DH, DH), DH)
            given_ref[d, :, :DH], given_ref[d, :, DH:] = wk_v[at], wv_v[at]

    load_tokens(step).wait()
    o_hi, o_lo = split(obs_v[step])
    kv = mm(o_hi, w_hi[...]) + mm(o_hi, w_lo[...]) + mm(o_lo, w_hi[...])
    hi, lo = split(kv)
    kv_ref[:, : 2 * DH], kv_ref[:, 2 * DH :] = hi, lo

    @pl.when(step == 0)
    def _():
        loads[2].wait()
        loads[3].wait()
        top, bottom = split(dot3(lat_v[...], wq_v[...]) * scale)
        q3[:, :DH], q3[:, DH : 2 * DH], q3[:, 2 * DH :] = top, top, bottom
        loads[4].wait()
        loads[5].wait()
        top, bottom = split(dot3(dout_v[...], wo_v[...], 1, 1))
        g3[:, :DH], g3[:, DH : 2 * DH], g3[:, 2 * DH :] = top, top, bottom

    scores, dprobs = scores_of(kv_ref, q3, g3)
    top = jnp.max(scores, axis=0, keepdims=True)
    expo = jnp.exp(scores - top)
    total = jnp.sum(expo, axis=0, keepdims=True)
    mix = jnp.sum(expo * dprobs, axis=0, keepdims=True)

    @pl.when(step == 0)
    def _():
        stat_ref[0:1], stat_ref[1:2], stat_ref[2:3] = top, total, mix

    @pl.when(step > 0)
    def _():
        before = stat_ref[0:1]
        now = jnp.maximum(before, top)
        w_before, w_new = jnp.exp(before - now), jnp.exp(top - now)
        stat_ref[0:1] = now
        stat_ref[1:2] = stat_ref[1:2] * w_before + total * w_new
        stat_ref[2:3] = stat_ref[2:3] * w_before + mix * w_new

    @pl.when(step == pl.num_programs(0) - 1)
    def _():
        sent_ref[...] = jnp.broadcast_to(stat_ref[...][None], sent_ref.shape)


def forward(n_ctx, core, *arrays):
    latents, d_out, w_query, w_out, w_key, w_value, observations = arrays
    lat, tok, width = latents.shape[0], observations.shape[0], observations.shape[1]
    steps = tok // CHUNK
    nx = width // DH // 2
    block = lambda cols: pl.BlockSpec((CHUNK, cols), lambda i: (i, 0))
    full = lambda *dims: pl.BlockSpec(dims, lambda i: (0,) * len(dims))
    return pl.pallas_call(
        lambda *refs: forward_kernel(1.0 / math.sqrt(DH), *refs),
        grid=(steps,),
        in_specs=[SCALARS] + [HBM] * 7,
        out_specs=[
            block(4 * DH), full(lat, 3 * DH), full(lat, 3 * DH),
            full(n_ctx, 3, lat), full(3, lat), full(nx, DH, 2 * DH),
        ],
        out_shape=[
            shape(tok, 4 * DH, dtype=BF16),
            shape(lat, 3 * DH, dtype=BF16), shape(lat, 3 * DH, dtype=BF16),
            shape(n_ctx, 3, lat), shape(3, lat), shape(nx, DH, 2 * DH),
        ],
        scratch_shapes=[
            VMEM(latents.shape, F32), VMEM(d_out.shape, F32), VMEM(w_query.shape, F32),
            VMEM(w_out.shape, F32), VMEM(w_key.shape, F32), VMEM(w_value.shape, F32),
            VMEM((steps, CHUNK, width), F32),
            pltpu.SemaphoreType.DMA((6,)), pltpu.SemaphoreType.DMA((steps,)),
            VMEM((width, 2 * DH), BF16), VMEM((width, 2 * DH), BF16),
        ],
        compiler_params=params(60),
        cost_estimate=cost(tok * width * 256 + 2 * tok * lat * DH, 18 << 20),
        name="forward",
    )(core, *[pin(a, pltpu.HBM) for a in arrays])


def grads_kernel(scale, mark_ref, stats_ref, kv_ref, q3, g3, out_ref, rows_ref, stat, acc):
    step = pl.program_id(0)

    @pl.when(step == 0)
    def _():
        tops = stats_ref[:, 0, :]
        top = jnp.max(tops, axis=0, keepdims=True)
        weight = jnp.exp(tops - top)
        total = jnp.sum(weight * stats_ref[:, 1, :], axis=0, keepdims=True)
        mix = jnp.sum(weight * stats_ref[:, 2, :], axis=0, keepdims=True)
        stat[0:1], stat[1:2], stat[2:3] = top, 1.0 / total, mix / total

    scores, dprobs = scores_of(kv_ref, q3, g3)
    probs = jnp.exp(scores - stat[0:1]) * stat[1:2]
    dscores = probs * (dprobs - stat[2:3])
    for at, value, packed in ((0, dscores, q3), (DH, probs, g3)):
        hi, lo = split(value)
        both = mm(hi, packed[:, DH:])
        out_ref[:, at : at + DH] = both[:, :DH] + both[:, DH:] + mm(lo, packed[:, :DH])
        t_hi, t_lo = kv_ref[:, at : at + DH], kv_ref[:, 2 * DH + at : 3 * DH + at]
        both = mm(jnp.concatenate([t_hi, t_lo], axis=1), hi, 0, 0)
        sums = both[:DH] + both[DH:] + mm(t_hi, lo, 0, 0)
        acc[at : at + DH] = jnp.where(step == 0, sums, acc[at : at + DH] + sums)

    @pl.when(step == pl.num_programs(0) - 1)
    def _():
        rows_ref[:, :DH] = acc[:DH].T * scale
        rows_ref[:, DH:] = acc[DH:].T


def token_grads(mark, stats, kv, q3, g3):
    tok, lat = kv.shape[0], q3.shape[0]
    return pl.pallas_call(
        lambda *refs: grads_kernel(1.0 / math.sqrt(DH), *refs),
        grid=(tok // CHUNK,),
        in_specs=[WHOLE, WHOLE, pl.BlockSpec((CHUNK, 4 * DH), lambda i: (i, 0)), WHOLE, WHOLE],
        out_specs=[
            pl.BlockSpec((CHUNK, 2 * DH), lambda i: (i, 0)),
            pl.BlockSpec((lat, 2 * DH), lambda i: (0, 0)),
        ],
        out_shape=[shape(tok, 2 * DH), shape(lat, 2 * DH)],
        scratch_shapes=[VMEM((3, lat), F32), VMEM((2 * DH, lat), F32)],
        compiler_params=params(60),
        cost_estimate=cost(6 * tok * lat * DH, 6 << 20),
        name="token_grads",
    )(mark, stats, kv, q3, g3)


def project(own, other, w):
    o_hi, o_lo = split(own)
    t_hi, t_lo = split(other)
    hi = jnp.concatenate([o_hi, t_hi], axis=1)
    lo = jnp.concatenate([o_lo, t_lo], axis=1)
    both = mm(hi, w, 1, 1)
    return both[:, :DH] + both[:, DH:] + mm(lo, w[:DH], 1, 1)


def first_kernel(own_a, other_a, own_b, other_b, far, near, back, right_ref, left_ref):
    a, b = (own_a[...], other_a[...]), (own_b[...], other_b[...])
    right_ref[0] = project(*a, far[0])
    right_ref[1] = project(*b, near[0])
    left_ref[0] = project(*b, far[0])
    left_ref[1] = project(*a, back[0])


def rest_kernel(own_a, other_a, own_b, other_b, home, near, back, right_ref, left_ref, out_ref):
    a, b = (own_a[...], other_a[...]), (own_b[...], other_b[...])
    right_ref[...] = project(*a, near[0])
    left_ref[...] = project(*b, back[0])
    out_ref[0] = project(*a, home[0])
    out_ref[1] = project(*b, home[0])


def token_part(kernel, own, other, w, which, outs, name, mib):
    half = own.shape[0] // 2
    steps = half // CHUNK
    a = pl.BlockSpec((CHUNK, 2 * DH), lambda i: (i, 0))
    b = pl.BlockSpec((CHUNK, 2 * DH), lambda i: (i + steps, 0))
    pair = pl.BlockSpec((2, CHUNK, DH), lambda i: (0, i, 0))
    one = pl.BlockSpec((CHUNK, DH), lambda i: (i, 0))
    chosen = [pl.BlockSpec((1,) + w.shape[1:], lambda i, k=k: (k, 0, 0)) for k in which]
    return pl.pallas_call(
        kernel,
        grid=(steps,),
        in_specs=[a, a, b, b] + chosen,
        out_specs=[pair if len(o.shape) == 3 else one for o in outs],
        out_shape=outs,
        compiler_params=params(mib),
        cost_estimate=cost(4 * half * 4 * DH * DH, 6 << 20),
        name=name,
    )(own, other, own, other, *[w] * len(which))


def weights_kernel(y_ref, obs_ref, joined_ref, o0, o1, o2, o3, acc, blocks):
    step = pl.program_id(0)
    joined = joined_ref[...]
    j_hi, j_lo = split(joined)
    o_hi, o_lo = split(obs_ref[...])
    value = mm(j_hi, o_hi, 0, 0) + mm(j_lo, o_hi, 0, 0) + mm(j_hi, o_lo, 0, 0)

    @pl.when(step == 0)
    def _():
        acc[...] = value

    @pl.when(step > 0)
    def _():
        acc[...] += value

    @pl.when(step == pl.num_programs(0) - 1)
    def _():
        nz, own = o0.shape[0], o0.shape[1]
        for i in range(nz):
            group = acc[:, i * NY * own : (i + 1) * NY * own].T
            blocks[i] = group.reshape(NY, own, 2 * DH)
        for k, out in enumerate((o0, o1, o2, o3)):
            out[...] = blocks[:, lax.rem(y_ref[0] + k, NY)]


def weight_grads(y, nz, observations, joined):
    tok, width = observations.shape
    own = width // nz // NY
    return pl.pallas_call(
        weights_kernel,
        grid=(tok // CHUNK,),
        in_specs=[
            SCALARS,
            pl.BlockSpec((CHUNK, width), lambda i: (i, 0)),
            pl.BlockSpec((CHUNK, 2 * DH), lambda i: (i, 0)),
        ],
        out_specs=[pl.BlockSpec((nz, own, 2 * DH), lambda i: (0, 0, 0))] * NY,
        out_shape=[shape(nz, own, 2 * DH)] * NY,
        scratch_shapes=[VMEM((2 * DH, width), F32), VMEM((nz, NY, own, 2 * DH), F32)],
        compiler_params=params(60),
        cost_estimate=cost(tok * width * 2 * DH, 11 << 20),
        name="weight_grads",
    )(y, observations, joined)


def small_call(kernel, outs, operands, scalars, after=(), scratch=(), name=None):
    def body(*refs):
        kernel(*refs[len(after) :])

    return pl.pallas_call(
        body,
        in_specs=[ANY] * len(after) + [SCALARS] * len(scalars) + [WHOLE] * len(operands),
        out_specs=[WHOLE] * len(outs),
        out_shape=list(outs),
        scratch_shapes=list(scratch),
        compiler_params=params(24),
        cost_estimate=cost(1 << 20, 1 << 20),
        name=name,
    )(*after, *scalars, *operands)


def loaded_call(kernel, outs, operands, scalars, after=(), mib=24, name=None):
    n_skip, n_scalars, n = len(after), len(scalars), len(operands)

    def body(*refs):
        refs = refs[n_skip:]
        sources, others = refs[n_scalars : n_scalars + n], refs[n_scalars + n :]
        results, buffers, sems = others[: len(outs)], others[len(outs) : -1], others[-1]
        loads = [
            pltpu.make_async_copy(source, buffer, sems.at[i])
            for i, (source, buffer) in enumerate(zip(sources, buffers))
        ]
        for load in loads:
            load.start()
        for load in loads:
            load.wait()
        kernel(*refs[:n_scalars], *buffers, *results)

    return pl.pallas_call(
        body,
        in_specs=[ANY] * n_skip + [SCALARS] * n_scalars + [ANY] * n,
        out_specs=[WHOLE] * len(outs),
        out_shape=list(outs),
        scratch_shapes=[VMEM(a.shape, a.dtype) for a in operands]
        + [pltpu.SemaphoreType.DMA((n,))],
        compiler_params=params(mib),
        cost_estimate=cost(1 << 20, 1 << 20),
        name=name,
    )(*after, *scalars, *operands)


def chip_weights_kernel(place_ref, wk_ref, wv_ref, taken_ref, out_ref, mark_ref):
    x, core = place_ref[0], place_ref[1]
    mark_ref[...] = jnp.zeros_like(mark_ref)
    nx = out_ref.shape[0]
    for r in range(nx):
        d = lax.rem(x + r, nx)
        at = pl.ds(pl.multiple_of((2 * d + core) * DH, DH), DH)
        pieces = (wk_ref[at], wv_ref[at], taken_ref[d, :, :DH], taken_ref[d, :, DH:])
        for i, piece in enumerate(pieces):
            hi, lo = split(piece)
            cols = slice(i * DH, (i + 1) * DH)
            out_ref[r, :DH, cols], out_ref[r, DH:, cols] = hi, lo


def second_kernel(near, back, from_left, from_right, right_ref, left_ref):
    right_ref[...] = near[...] + from_left[0]
    left_ref[...] = back[...] + from_right[0]


def last_kernel(home, left1, right1, left2, right2, out_ref, mark_ref):
    mark_ref[...] = jnp.zeros_like(mark_ref)
    half = home.shape[1]
    out_ref[:half] = home[0] + left2[...] + right1[1]
    out_ref[half:] = home[1] + left1[1] + right2[...]


def latent_part_kernel(both_ref, wq_ref, rows_ref, part_ref):
    rows = jnp.sum(both_ref[...], axis=0)
    rows_ref[...] = rows
    part = dot3(rows[:, :DH], wq_ref[...], 1, 1)
    for h in range(part_ref.shape[0]):
        part_ref[h] = part[:, h * DH : (h + 1) * DH]


def latent_rows_kernel(rows_ref, part_ref, w0, w1, w2, w3, out_ref):
    d_lat = jnp.sum(part_ref[...], axis=0)
    half = out_ref.shape[1]
    for i in range(out_ref.shape[0]):
        out_ref[i, :, : 2 * DH] = rows_ref[...]
        out_ref[i, :, 2 * DH : 3 * DH] = d_lat
        weights = (w0[i] + w1[i]) + (w2[i] + w3[i])
        out_ref[i, :, 3 * DH : 5 * DH] = weights[:half]
        out_ref[i, :, 5 * DH :] = weights[half:]


def gathered_kernel(got_ref, rows_ref, key_ref, value_ref):
    half = got_ref.shape[1]
    total = got_ref[0, :, 3 * DH :]
    for i in range(1, got_ref.shape[0]):
        total += got_ref[i, :, 3 * DH :]
    for i in range(got_ref.shape[0]):
        rows_ref[i * half : (i + 1) * half] = got_ref[i, :, : 3 * DH]
    key_ref[:half], key_ref[half:] = total[:, :DH], total[:, 2 * DH : 3 * DH]
    value_ref[:half], value_ref[half:] = total[:, DH : 2 * DH], total[:, 3 * DH :]


def final_kernel(y_ref, _, own, r1, r2, r3, lat_ref, dout_ref, d_lat_ref, d_wq_ref, d_wo_ref, all_rows):
    nz, rows = all_rows.shape[0], all_rows.shape[2]
    for k, part in enumerate((own, r1, r2, r3)):
        all_rows[:, lax.rem(y_ref[0] + NY - k, NY)] = part[...].reshape(nz, rows, 3 * DH)
    both = all_rows[...].reshape(d_lat_ref.shape[0], 3 * DH)
    d_lat_ref[...] = both[:, 2 * DH :]
    d_wq_ref[...] = dot3(lat_ref[...], both[:, :DH], 0, 0)
    d_wo_ref[...] = dot3(both[:, DH : 2 * DH], dout_ref[...], 0, 0)


def on_device(latents, observations, w_query, w_key, w_value, w_out, d_out):
    lat = latents.shape[0]
    width = observations.shape[1]
    n_ctx, n_head = lax.axis_size("ctx"), lax.axis_size("head")
    nz, nx = n_ctx // NY, n_head // 2
    ctx, head = lax.axis_index("ctx"), lax.axis_index("head")
    z, y = ctx // NY, ctx % NY
    x, core = head // 2, head % 2
    z_groups = [[a * NY + b for a in range(nz)] for b in range(NY)]
    swap = [(i, i ^ 1) for i in range(n_head)]
    right = [(i, (i + 2) % n_head) for i in range(n_head)]
    left = [(i, (i - 2) % n_head) for i in range(n_head)]
    rows_z = lat // n_ctx
    rows_y = rows_z * nz

    def along_y(k):
        return [(i, i - i % NY + (i + k) % NY) for i in range(n_ctx)]

    kv, q3, g3, sent, stat, given = forward(
        n_ctx, core.reshape(1), latents, d_out, w_query, w_out, w_key, w_value, observations
    )
    stats = lax.all_to_all(sent, "ctx", 0, 0)
    taken = lax.ppermute(given, "head", swap)
    w_chip, mark = small_call(
        chip_weights_kernel, [shape(nx, 2 * DH, 4 * DH, dtype=BF16), shape(8, DH)],
        [w_key, w_value, taken], [jnp.stack([x, core])], name="chip_weights",
    )
    own, rows = token_grads(mark, stats, kv, q3, g3)

    half = own.shape[0] // 2
    other = lax.ppermute(own, "head", swap)
    rows = lax.all_to_all(rows.reshape(n_ctx, rows_z, 2 * DH), "ctx", 0, 0)
    d_w = weight_grads(y.reshape(1), nz, observations, own)
    d_w = [d_w[0]] + [lax.ppermute(d_w[k], "ctx", along_y(k)) for k in range(1, NY)]
    right_1, left_1 = token_part(
        first_kernel, own, other, w_chip, (2, 1, 3), [shape(2, half, DH)] * 2, "token_first", 60
    )
    from_left_1 = lax.ppermute(right_1, "head", right)
    from_right_1 = lax.ppermute(left_1, "head", left)
    near, back, home = token_part(
        rest_kernel, own, other, w_chip, (0, 1, 3),
        [shape(half, DH), shape(half, DH), shape(2, half, DH)], "token_rest", 24,
    )

    rows, part = loaded_call(
        latent_part_kernel, [shape(rows_z, 2 * DH), shape(n_head, rows_z, DH)],
        [rows, w_query], [], name="latent_part",
    )
    part = lax.all_to_all(part, "head", 0, 0)
    (sent,) = small_call(
        latent_rows_kernel, [shape(nz, rows_z, 7 * DH)], [rows, part, *d_w], [],
        name="latent_rows",
    )
    got = lax.all_to_all(sent, "ctx", 0, 0, axis_index_groups=z_groups)
    right_2, left_2 = small_call(
        second_kernel, [shape(half, DH)] * 2, [near, back, from_left_1, from_right_1], [],
        name="token_second",
    )
    from_left_2 = lax.ppermute(right_2, "head", right)
    from_right_2 = lax.ppermute(left_2, "head", left)
    rows, d_w_key, d_w_value = small_call(
        gathered_kernel,
        [shape(rows_y, 3 * DH), shape(width // n_ctx, DH), shape(width // n_ctx, DH)],
        [got], [], name="gathered",
    )
    rows = [rows] + [lax.ppermute(rows, "ctx", along_y(k)) for k in range(1, NY)]
    d_observations, mark = small_call(
        last_kernel, [shape(2 * half, DH), shape(8, DH)],
        [home, from_left_1, from_right_1, from_left_2, from_right_2], [], name="token_last",
    )
    d_latents, d_w_query, d_w_out = small_call(
        final_kernel, [shape(lat, DH), shape(width, DH), shape(DH, width)],
        [mark, *rows, latents, d_out], [y.reshape(1)],
        scratch=[VMEM((nz, NY, rows_z, 3 * DH), F32)], name="final",
    )
    return (d_latents, d_observations, d_w_query, d_w_key, d_w_value, d_w_out)


def solution(mesh):
    placed = (
        P(),
        P("ctx", None),
        P(None, "head"),
        P(None, "head"),
        P(None, "head"),
        P("head", None),
        P(),
    )
    return jax.shard_map(
        on_device,
        mesh=mesh,
        in_specs=placed,
        out_specs=(
            P(None, "head"),
            P("ctx", "head"),
            P(None, "head"),
            P("ctx", "head"),
            P("ctx", "head"),
            P("head", None),
        ),
        check_vma=False,
    )
```

time: 153 us -> 135 us (0.88)
  local copies, waits for them, and re-layouts: 26.7 us -> 8.92 us
  starting transfers between devices: 50.7 us -> 45.1 us
  waiting for transfers between devices: 21.7 us -> 24.7 us
  Pallas kernels: 51.3 us -> 53.2 us
    unnamed x62 -> x32, local copies, waits for them, and re-layouts: 26.7 us -> 8.92 us
    all_to_all x1, waiting for transfers between devices: 0.01 us -> 9.59 us  [on_device(): stats = lax.all_to_all(sent, 'ctx', 0, 0)]
    ppermute x3, waiting for transfers between devices: 8.59 us -> 4.06 us  [on_device(): lax.ppermute(rows, 'ctx', along_y(k))]
    ppermute x5 -> x1, starting transfers between devices: 5.59 us -> 2 us  [on_device(): other = lax.ppermute(own, 'head', swap)]
    pallas_call x7 -> x6, Pallas kernels: 7.73 us -> 10.5 us  [small_call(): pl.pallas_call(body, in_specs=[ANY] * len(after) + [SCALARS] * len(scalar...]
    all_to_all x1, starting transfers between devices: 6.93 us -> 4.89 us  [on_device(): part = lax.all_to_all(part, 'head', 0, 0)]
    all_to_all x1, starting transfers between devices: 6.38 us -> 4.62 us  [on_device(): rows = lax.all_to_all(rows.reshape(n_ctx, rows_z, 2 * DH), 'ctx', 0, 0)]
    ppermute x5 -> x1, waiting for transfers between devices: 1.76 us -> 0.01 us  [on_device(): other = lax.ppermute(own, 'head', swap)]
  transfers between devices with their start and end apart: 20 -> 16, of which waited for: 6 -> 6; matrix products, arithmetic and copies ran while one was open for 0% -> 0% of each run, Pallas kernels for 18% -> 20%
where the time goes in v2:
time: 135 us; the launch traced here: 133 us
  Pallas kernels  53.2 us (39%)
  starting transfers between devices  45.1 us (33%)
  waiting for transfers between devices  24.7 us (18%)
  local copies, waits for them, and re-layouts  8.92 us (7%)
    pallas_call x1, Pallas kernels, forward(): pl.pallas_call(lambda *refs: forward_kernel(1.0 / math.sqrt(DH), *refs),...  14.6 us
    pallas_call x6, Pallas kernels, small_call(): pl.pallas_call(body, in_specs=[ANY] * len(after) + [SCALARS] * len(scalar...  10.5 us
    pallas_call x1, Pallas kernels, token_grads(): pl.pallas_call(lambda *refs: grads_kernel(1.0 / math.sqrt(DH), *refs), gr...  9.79 us
    all_to_all x1, waiting for transfers between devices, on_device(): stats = lax.all_to_all(sent, 'ctx', 0, 0)  9.59 us
    all_to_all x1, starting transfers between devices, on_device(): stats = lax.all_to_all(sent, 'ctx', 0, 0)  9.47 us
    unnamed x32, local copies, waits for them, and re-layouts  8.92 us
    pallas_call x1, Pallas kernels, weight_grads(): pl.pallas_call(weights_kernel, grid=(tok // CHUNK,), in_specs=[SCALARS, p...  8.13 us
    pallas_call x2, Pallas kernels, token_part(): pl.pallas_call(kernel, grid=(steps,), in_specs=[a, a, b, b] + chosen, out...  8.12 us
  transfers between devices with their start and end apart: 16, of which 6 were waited for; matrix products, arithmetic and copies ran while one was open for 0% of the time, Pallas kernels for 20%

profile of v2, /device:TPU:1, one launch (start us, length us, event | category | flops | bytes accessed | tf_op | source)
XLA Modules:
  0.0 132.7 jit_solution(2148356013778877329)
XLA Ops:
  0.7 14.6 %forward.1 = (bf16[2048,512]{1,0:T(8,128)(2,1)}, bf16[512,384]{1,0:T(8,128)(2,1)}, bf16[512,384]{1,0:T(8,128)(2,1)}, f32[32,3,512]{2,1,0:T(4,128)}, f32[3,512]{1,0:T(4,128)}, /*index=5*/f32[4,128,256]{2,1,0:T(8,128)}) custom-call(s32[1]{0:T(128)} %bitcast.2.refs_0_, f32[512,1024]{1,0:T(8,128)} %refs_6_.3, f32[512,1024]{1,0:T(8,128)} %refs_7_.3, ...), custom_call_target="tpu_custom_call" | custom-call | flops 4831838208 | bytes 18874368 | tf_op jit(solution)/shard_map/forward/pallas_call | solution.py:146
  15.2 3.3 %collective-permute-start = (f32[4,128,256]{2,1,0:T(8,128)}, f32[4,128,256]{2,1,0:T(8,128)S(1)}, u32[]{:S(2)}, u32[]{:S(2)}) collective-permute-start(f32[4,128,256]{2,1,0:T(8,128)} %get-tuple-element.36), channel_id=1, source_target_pairs={{0,1},{1,0},{2,3},{3,2},{4,5},{5,4},{6,7},{7,6},{8,9},{9,8},{10,11... | collective-permute-start | bytes 1572872 | tf_op jit(solution)/shard_map/ppermute | solution.py:444
  18.6 9.5 %all-to-all-start = ((f32[32,3,512]{2,1,0:T(4,128)}), f32[32,3,512]{2,1,0:T(4,128)S(1)}, u32[]{:S(2)}, u32[]{:S(2)}) async-start(f32[32,3,512]{2,1,0:T(4,128)} %get-tuple-element.38), calls=%async_computation | async-start | bytes 524288 | tf_op jit(solution)/shard_map/all_to_all | solution.py:443
  30.4 9.6 %all-to-all-done.refs_1_ = f32[32,3,512]{2,1,0:T(4,128)S(1)} async-done(((f32[32,3,512]{2,1,0:T(4,128)}), f32[32,3,512]{2,1,0:T(4,128)S(1)}, u32[]{:S(2)}, u32[]{:S(2)}) %all-to-all-start) | async-done | bytes 196640 | tf_op jit(solution)/shard_map/all_to_all | solution.py:443
  40.7 9.8 %token_grads.1 = (f32[2048,256]{1,0:T(8,128)}, f32[512,256]{1,0:T(8,128)}) custom-call(f32[8,128]{1,0:T(8,128)} %copy-done.14, f32[32,3,512]{2,1,0:T(4,128)} %copy-done.15, bf16[2048,512]{1,0:T(8,128)(2,1)} %get-tuple-element.39.refs_2_, bf16[512,384]{1,0:T(8,128)(2,1)} %get-tuple-element.40.refs_3_, bf16[512,384]{1,0:T(8,128)(2,1)} %get-tuple-element.41.refs_4_), custom_call_target="tpu_custom_call" | custom-call | flops 4831838208 | bytes 6291456 | tf_op jit(solution)/shard_map/token_grads/pallas_call | solution.py:204
  50.5 2.0 %collective-permute-start.1 = (f32[2048,256]{1,0:T(8,128)}, f32[2048,256]{1,0:T(8,128)S(1)}, u32[]{:S(2)}, u32[]{:S(2)}) collective-permute-start(f32[2048,256]{1,0:T(8,128)} %get-tuple-element.42.own_a.own_b.joined_ref), channel_id=1, source_target_pairs={{0,1},{1,0},{2,3},{3,2},{4,5},{5,4},{6,7},{7,6},{8,9},{9,8},{10,11... | collective-permute-start | bytes 6291464 | tf_op jit(solution)/shard_map/ppermute | solution.py:452
  52.5 4.6 %all-to-all-start.1 = ((f32[32,16,256]{2,1,0:T(8,128)}), f32[32,16,256]{2,1,0:T(8,128)}, u32[]{:S(2)}, u32[]{:S(2)}) async-start(f32[32,16,256]{2,1,0:T(8,128)} %bitcast.4), calls=%async_computation.1 | async-start | bytes 1048576 | tf_op jit(solution)/shard_map/all_to_all | solution.py:453
  58.5 5.5 %token_first.1 = (f32[2,1024,128]{2,1,0:T(8,128)}, f32[2,1024,128]{2,1,0:T(8,128)}) custom-call(f32[2048,256]{1,0:T(8,128)} %get-tuple-element.42.own_a.own_b.joined_ref, f32[2048,256]{1,0:T(8,128)} %copy-done.3, f32[2048,256]{1,0:T(8,128)} %get-tuple-element.42.own_a.own_b.joined_ref, f32[2048,256]{1,0:T(8,128)} %copy-done.3, bf16[4,256,512]{2,1,0:T(8,128)(2,1)} %copy-done, ...), custom_call_target="tpu_custom_call" | custom-call | flops 1610612736 | bytes 6291456 | tf_op jit(solution)/shard_map/token_first/pallas_call | solution.py:253
  66.8 8.1 %weight_grads.1 = (f32[8,32,256]{2,1,0:T(8,128)}, f32[8,32,256]{2,1,0:T(8,128)}, f32[8,32,256]{2,1,0:T(8,128)}, f32[8,32,256]{2,1,0:T(8,128)}) custom-call(s32[1]{0:T(128)} %bitcast.y_ref.refs_0_, f32[2048,1024]{1,0:T(8,128)} %obs_ref.1, f32[2048,256]{1,0:T(8,128)} %get-tuple-element.42.own_a.own_b.joined_ref), custom_call_target="tpu_custom_call" | custom-call | flops 3221225472 | bytes 11534336 | tf_op jit(solution)/shard_map/weight_grads/pallas_call | solution.py:293
  76.0 2.4 %collective-permute-start.7 = (f32[8,32,256]{2,1,0:T(8,128)}, f32[8,32,256]{2,1,0:T(8,128)}, u32[]{:S(2)}, u32[]{:S(2)}) collective-permute-start(f32[8,32,256]{2,1,0:T(8,128)} %get-tuple-element.57), channel_id=1, source_target_pairs={{0,16},{8,24},{16,0},{24,8},{32,48},{40,56},{48,32},{56,40},{64,80... | collective-permute-start | bytes 786440 | tf_op jit(solution)/shard_map/ppermute | solution.py:455
  80.6 2.0 %latent_part.1 = (f32[16,256]{1,0:T(8,128)S(1)}, f32[8,16,128]{2,1,0:T(8,128)}) custom-call(f32[32,16,256]{2,1,0:T(8,128)} %all-to-all-done.1.refs_0_, f32[1024,128]{1,0:T(8,128)S(1)} %copy-done.12), custom_call_target="tpu_custom_call" | custom-call | flops 6291456 | bytes 1048576 | tf_op jit(solution)/shard_map/latent_part/pallas_call | solution.py:343
  82.7 4.9 %all-to-all-start.2 = ((f32[8,16,128]{2,1,0:T(8,128)}), f32[8,16,128]{2,1,0:T(8,128)S(1)}, u32[]{:S(2)}, u32[]{:S(2)}) async-start(f32[8,16,128]{2,1,0:T(8,128)} %get-tuple-element.54), calls=%async_computation.2 | async-start | bytes 131072 | tf_op jit(solution)/shard_map/all_to_all | solution.py:470
  87.6 2.3 %collective-permute-done.7.refs_4_ = f32[8,32,256]{2,1,0:T(8,128)} collective-permute-done((f32[8,32,256]{2,1,0:T(8,128)}, f32[8,32,256]{2,1,0:T(8,128)}, u32[]{:S(2)}, u32[]{:S(2)}) %collective-permute-start.7) | collective-permute-done | bytes 262176 | tf_op jit(solution)/shard_map/ppermute | solution.py:455
  89.9 2.5 %all-to-all-done.2.refs_1_ = f32[8,16,128]{2,1,0:T(8,128)S(1)} async-done(((f32[8,16,128]{2,1,0:T(8,128)}), f32[8,16,128]{2,1,0:T(8,128)S(1)}, u32[]{:S(2)}, u32[]{:S(2)}) %all-to-all-start.2) | async-done | bytes 65568 | tf_op jit(solution)/shard_map/all_to_all | solution.py:470
  95.3 6.5 %all-to-all-start.3 = ((f32[8,16,896]{2,1,0:T(8,128)}), f32[8,16,896]{2,1,0:T(8,128)}, u32[]{:S(2)}, u32[]{:S(2)}) async-start(f32[8,16,896]{2,1,0:T(8,128)} %copy-done.7), calls=%async_computation.3 | async-start | bytes 917504 | tf_op jit(solution)/shard_map/all_to_all | solution.py:475
  103.4 2.6 %token_rest.1 = (f32[1024,128]{1,0:T(8,128)S(1)}, f32[1024,128]{1,0:T(8,128)S(1)}, f32[2,1024,128]{2,1,0:T(8,128)S(1)}) custom-call(f32[2048,256]{1,0:T(8,128)S(1)} %copy-done.2, f32[2048,256]{1,0:T(8,128)S(1)} %copy-done.4, f32[2048,256]{1,0:T(8,128)S(1)} %copy-done.2, f32[2048,256]{1,0:T(8,128)S(1)} %copy-done.4, bf16[4,256,512]{2,1,0:T(8,128)(2,1)S(1)} %copy-done.1, ...), custom_call_target="tpu_custom_call" | custom-call | flops 1610612736 | bytes 6291456 | tf_op jit(solution)/shard_map/token_rest/pallas_call | solution.py:253
  107.0 1.7 %token_second.1 = (f32[1024,128]{1,0:T(8,128)S(1)}, f32[1024,128]{1,0:T(8,128)S(1)}) custom-call(f32[1024,128]{1,0:T(8,128)S(1)} %get-tuple-element.47.refs_0_, f32[1024,128]{1,0:T(8,128)S(1)} %get-tuple-element.48.refs_1_, f32[2,1024,128]{2,1,0:T(8,128)} %collective-permute-done.2.refs_2_.refs_1_, f32[2,1024,128]{2,1,0:T(8,128)} %collective-permute-done.3.refs_3_.refs_2_), custom_call_target="tpu_custom_call" | custom-call | flops 6291456 | bytes 1048576 | tf_op jit(solution)/shard_map/token_second/pallas_call | solution.py:314
  109.1 2.4 %collective-permute-start.5 = (f32[1024,128]{1,0:T(8,128)S(1)}, f32[1024,128]{1,0:T(8,128)S(1)}, u32[]{:S(2)}, u32[]{:S(2)}) collective-permute-start(f32[1024,128]{1,0:T(8,128)S(1)} %get-tuple-element.50), channel_id=1, source_target_pairs={{0,6},{1,7},{2,0},{3,1},{4,2},{5,3},{6,4},{7,5},{8,14},{9,15},{10,... | collective-permute-start | bytes 1572872 | tf_op jit(solution)/shard_map/ppermute | solution.py:481
  111.4 6.1 %all-to-all-done.3.refs_0_ = f32[8,16,896]{2,1,0:T(8,128)} async-done(((f32[8,16,896]{2,1,0:T(8,128)}), f32[8,16,896]{2,1,0:T(8,128)}, u32[]{:S(2)}, u32[]{:S(2)}) %all-to-all-start.3) | async-done | bytes 458784 | tf_op jit(solution)/shard_map/all_to_all | solution.py:475
  117.6 1.6 %gathered.1 = (f32[128,384]{1,0:T(8,128)S(1)}, f32[32,128]{1,0:T(8,128)}, f32[32,128]{1,0:T(8,128)}) custom-call(f32[8,16,896]{2,1,0:T(8,128)} %all-to-all-done.3.refs_0_), custom_call_target="tpu_custom_call" | custom-call | flops 6291456 | bytes 1048576 | tf_op jit(solution)/shard_map/gathered/pallas_call | solution.py:314
  119.7 2.4 %collective-permute-start.10 = (f32[128,384]{1,0:T(8,128)S(1)}, f32[128,384]{1,0:T(8,128)S(1)}, u32[]{:S(2)}, u32[]{:S(2)}) collective-permute-start(f32[128,384]{1,0:T(8,128)S(1)} %get-tuple-element.59.refs_2_), channel_id=1, source_target_pairs={{0,16},{8,24},{16,0},{24,8},{32,48},{40,56},{48,32},{56,40},{64,80... | collective-permute-start | bytes 589832 | tf_op jit(solution)/shard_map/ppermute | solution.py:487
  123.4 2.8 %token_last.1 = (f32[2048,128]{1,0:T(8,128)}, f32[8,128]{1,0:T(8,128)S(1)}) custom-call(f32[2,1024,128]{2,1,0:T(8,128)S(1)} %copy-done.9, f32[2,1024,128]{2,1,0:T(8,128)} %collective-permute-done.2.refs_2_.refs_1_, f32[2,1024,128]{2,1,0:T(8,128)} %collective-permute-done.3.refs_3_.refs_2_, f32[1024,128]{1,0:T(8,128)S(1)} %collective-permute-done.4.refs_3_, ...), custom_call_target="tpu_custom_call" | custom-call | flops 6291456 | bytes 1048576 | tf_op jit(solution)/shard_map/token_last/pallas_call | solution.py:314
  126.2 3.8 %collective-permute-done.10.refs_4_ = f32[128,384]{1,0:T(8,128)S(1)} collective-permute-done((f32[128,384]{1,0:T(8,128)S(1)}, f32[128,384]{1,0:T(8,128)S(1)}, u32[]{:S(2)}, u32[]{:S(2)}) %collective-permute-start.10) | collective-permute-done | bytes 196640 | tf_op jit(solution)/shard_map/ppermute | solution.py:487
  130.3 2.5 %final.1 = (f32[512,128]{1,0:T(8,128)}, f32[1024,128]{1,0:T(8,128)}, f32[128,1024]{1,0:T(8,128)}) custom-call(s32[1]{0:T(128)} %bitcast.y_ref.refs_0_, f32[8,128]{1,0:T(8,128)S(1)} %get-tuple-element.51.refs_1_, f32[128,384]{1,0:T(8,128)S(1)} %get-tuple-element.59.refs_2_, f32[128,384]{1,0:T(8,128)S(1)} %collective-permute-done.9.refs_3_, ...), custom_call_target="tpu_custom_call" | custom-call | flops 6291456 | bytes 1048576 | tf_op jit(solution)/shard_map/final/pallas_call | solution.py:314
  (53 shorter events, 18.2 us)
Async XLA Ops:
  0.6 27.5 %copy-start.10 = (f32[1024,128]{1,0:T(8,128)S(1)}, f32[1024,128]{1,0:T(8,128)}, u32[]{:S(2)}) copy-start(f32[1024,128]{1,0:T(8,128)} %refs_1_.4) | copy-start | bytes 1572868
  0.7 27.5 %copy-start.11 = (f32[1024,128]{1,0:T(8,128)S(1)}, f32[1024,128]{1,0:T(8,128)}, u32[]{:S(2)}) copy-start(f32[1024,128]{1,0:T(8,128)} %refs_2_.3) | copy-start | bytes 1572868
  15.2 12.9 %collective-permute-start = (f32[4,128,256]{2,1,0:T(8,128)}, f32[4,128,256]{2,1,0:T(8,128)S(1)}, u32[]{:S(2)}, u32[]{:S(2)}) collective-permute-start(f32[4,128,256]{2,1,0:T(8,128)} %get-tuple-element.36), channel_id=1, source_target_pairs={{0,1},{1,0},{2,3},{3,2},{4,5},{5,4},{6,7},{7,6},{8,9},{9,8},{10,11... | collective-permute-start | bytes 1572872 | tf_op jit(solution)/shard_map/ppermute | solution.py:444
  18.6 21.5 %all-to-all-start = ((f32[32,3,512]{2,1,0:T(4,128)}), f32[32,3,512]{2,1,0:T(4,128)S(1)}, u32[]{:S(2)}, u32[]{:S(2)}) async-start(f32[32,3,512]{2,1,0:T(4,128)} %get-tuple-element.38), calls=%async_computation | async-start | bytes 524288 | tf_op jit(solution)/shard_map/all_to_all | solution.py:443
  50.5 6.6 %collective-permute-start.1 = (f32[2048,256]{1,0:T(8,128)}, f32[2048,256]{1,0:T(8,128)S(1)}, u32[]{:S(2)}, u32[]{:S(2)}) collective-permute-start(f32[2048,256]{1,0:T(8,128)} %get-tuple-element.42.own_a.own_b.joined_ref), channel_id=1, source_target_pairs={{0,1},{1,0},{2,3},{3,2},{4,5},{5,4},{6,7},{7,6},{8,9},{9,8},{10,11... | collective-permute-start | bytes 6291464 | tf_op jit(solution)/shard_map/ppermute | solution.py:452
  52.5 27.1 %all-to-all-start.1 = ((f32[32,16,256]{2,1,0:T(8,128)}), f32[32,16,256]{2,1,0:T(8,128)}, u32[]{:S(2)}, u32[]{:S(2)}) async-start(f32[32,16,256]{2,1,0:T(8,128)} %bitcast.4), calls=%async_computation.1 | async-start | bytes 1048576 | tf_op jit(solution)/shard_map/all_to_all | solution.py:453
  64.0 42.9 %collective-permute-start.2 = (f32[2,1024,128]{2,1,0:T(8,128)}, f32[2,1024,128]{2,1,0:T(8,128)}, u32[]{:S(2)}, u32[]{:S(2)}) collective-permute-start(f32[2,1024,128]{2,1,0:T(8,128)} %get-tuple-element.45), channel_id=1, source_target_pairs={{0,2},{1,3},{2,4},{3,5},{4,6},{5,7},{6,0},{7,1},{8,10},{9,11},{10,... | collective-permute-start | bytes 3145736 | tf_op jit(solution)/shard_map/ppermute | solution.py:459
  65.2 41.7 %collective-permute-start.3 = (f32[2,1024,128]{2,1,0:T(8,128)}, f32[2,1024,128]{2,1,0:T(8,128)}, u32[]{:S(2)}, u32[]{:S(2)}) collective-permute-start(f32[2,1024,128]{2,1,0:T(8,128)} %get-tuple-element.46), channel_id=1, source_target_pairs={{0,6},{1,7},{2,0},{3,1},{4,2},{5,3},{6,4},{7,5},{8,14},{9,15},{10,... | collective-permute-start | bytes 3145736 | tf_op jit(solution)/shard_map/ppermute | solution.py:460
  74.9 26.9 %copy-start.1 = (bf16[4,256,512]{2,1,0:T(8,128)(2,1)S(1)}, bf16[4,256,512]{2,1,0:T(8,128)(2,1)}, u32[]{:S(2)}) copy-start(bf16[4,256,512]{2,1,0:T(8,128)(2,1)} %copy-done) | copy-start | bytes 3145732
  74.9 26.9 %copy-start.2 = (f32[2048,256]{1,0:T(8,128)S(1)}, f32[2048,256]{1,0:T(8,128)}, u32[]{:S(2)}) copy-start(f32[2048,256]{1,0:T(8,128)} %get-tuple-element.42.own_a.own_b.joined_ref) | copy-start | bytes 6291460
  74.9 12.7 %collective-permute-start.6 = (f32[8,32,256]{2,1,0:T(8,128)}, f32[8,32,256]{2,1,0:T(8,128)S(1)}, u32[]{:S(2)}, u32[]{:S(2)}) collective-permute-start(f32[8,32,256]{2,1,0:T(8,128)} %get-tuple-element.56), channel_id=1, source_target_pairs={{0,8},{8,16},{16,24},{24,0},{32,40},{40,48},{48,56},{56,32},{64,72... | collective-permute-start | bytes 786440 | tf_op jit(solution)/shard_map/ppermute | solution.py:455
  76.0 13.9 %collective-permute-start.7 = (f32[8,32,256]{2,1,0:T(8,128)}, f32[8,32,256]{2,1,0:T(8,128)}, u32[]{:S(2)}, u32[]{:S(2)}) collective-permute-start(f32[8,32,256]{2,1,0:T(8,128)} %get-tuple-element.57), channel_id=1, source_target_pairs={{0,16},{8,24},{16,0},{24,8},{32,48},{40,56},{48,32},{56,40},{64,80... | collective-permute-start | bytes 786440 | tf_op jit(solution)/shard_map/ppermute | solution.py:455
  78.4 11.5 %collective-permute-start.8 = (f32[8,32,256]{2,1,0:T(8,128)}, f32[8,32,256]{2,1,0:T(8,128)}, u32[]{:S(2)}, u32[]{:S(2)}) collective-permute-start(f32[8,32,256]{2,1,0:T(8,128)} %get-tuple-element.58), channel_id=1, source_target_pairs={{0,24},{8,0},{16,8},{24,16},{32,56},{40,32},{48,40},{56,48},{64,88... | collective-permute-start | bytes 786440 | tf_op jit(solution)/shard_map/ppermute | solution.py:455
  82.7 9.8 %all-to-all-start.2 = ((f32[8,16,128]{2,1,0:T(8,128)}), f32[8,16,128]{2,1,0:T(8,128)S(1)}, u32[]{:S(2)}, u32[]{:S(2)}) async-start(f32[8,16,128]{2,1,0:T(8,128)} %get-tuple-element.54), calls=%async_computation.2 | async-start | bytes 131072 | tf_op jit(solution)/shard_map/all_to_all | solution.py:470
  95.3 22.3 %all-to-all-start.3 = ((f32[8,16,896]{2,1,0:T(8,128)}), f32[8,16,896]{2,1,0:T(8,128)}, u32[]{:S(2)}, u32[]{:S(2)}) async-start(f32[8,16,896]{2,1,0:T(8,128)} %copy-done.7), calls=%async_computation.3 | async-start | bytes 917504 | tf_op jit(solution)/shard_map/all_to_all | solution.py:475
  101.8 1.6 %copy-start.4 = (f32[2048,256]{1,0:T(8,128)S(1)}, f32[2048,256]{1,0:T(8,128)}, u32[]{:S(2)}) copy-start(f32[2048,256]{1,0:T(8,128)} %copy-done.3) | copy-start | bytes 6291460
  106.9 16.4 %copy-start.9 = (f32[2,1024,128]{2,1,0:T(8,128)S(1)}, f32[2,1024,128]{2,1,0:T(8,128)}, u32[]{:S(2)}) copy-start(f32[2,1024,128]{2,1,0:T(8,128)} %copy-done.8) | copy-start | bytes 3145732
  108.7 14.6 %collective-permute-start.4 = (f32[1024,128]{1,0:T(8,128)S(1)}, f32[1024,128]{1,0:T(8,128)S(1)}, u32[]{:S(2)}, u32[]{:S(2)}) collective-permute-start(f32[1024,128]{1,0:T(8,128)S(1)} %get-tuple-element.49), channel_id=1, source_target_pairs={{0,2},{1,3},{2,4},{3,5},{4,6},{5,7},{6,0},{7,1},{8,10},{9,11},{10,... | collective-permute-start | bytes 1572872 | tf_op jit(solution)/shard_map/ppermute | solution.py:480
  109.1 14.3 %collective-permute-start.5 = (f32[1024,128]{1,0:T(8,128)S(1)}, f32[1024,128]{1,0:T(8,128)S(1)}, u32[]{:S(2)}, u32[]{:S(2)}) collective-permute-start(f32[1024,128]{1,0:T(8,128)S(1)} %get-tuple-element.50), channel_id=1, source_target_pairs={{0,6},{1,7},{2,0},{3,1},{4,2},{5,3},{6,4},{7,5},{8,14},{9,15},{10,... | collective-permute-start | bytes 1572872 | tf_op jit(solution)/shard_map/ppermute | solution.py:481
  119.2 7.0 %collective-permute-start.9 = (f32[128,384]{1,0:T(8,128)S(1)}, f32[128,384]{1,0:T(8,128)S(1)}, u32[]{:S(2)}, u32[]{:S(2)}) collective-permute-start(f32[128,384]{1,0:T(8,128)S(1)} %get-tuple-element.59.refs_2_), channel_id=1, source_target_pairs={{0,8},{8,16},{16,24},{24,0},{32,40},{40,48},{48,56},{56,32},{64,72... | collective-permute-start | bytes 589832 | tf_op jit(solution)/shard_map/ppermute | solution.py:487
  119.7 10.2 %collective-permute-start.10 = (f32[128,384]{1,0:T(8,128)S(1)}, f32[128,384]{1,0:T(8,128)S(1)}, u32[]{:S(2)}, u32[]{:S(2)}) collective-permute-start(f32[128,384]{1,0:T(8,128)S(1)} %get-tuple-element.59.refs_2_), channel_id=1, source_target_pairs={{0,16},{8,24},{16,0},{24,8},{32,48},{40,56},{48,32},{56,40},{64,80... | collective-permute-start | bytes 589832 | tf_op jit(solution)/shard_map/ppermute | solution.py:487
  122.2 8.1 %collective-permute-start.11 = (f32[128,384]{1,0:T(8,128)S(1)}, f32[128,384]{1,0:T(8,128)S(1)}, u32[]{:S(2)}, u32[]{:S(2)}) collective-permute-start(f32[128,384]{1,0:T(8,128)S(1)} %get-tuple-element.59.refs_2_), channel_id=1, source_target_pairs={{0,24},{8,0},{16,8},{24,16},{32,56},{40,32},{48,40},{56,48},{64,88... | collective-permute-start | bytes 589832 | tf_op jit(solution)/shard_map/ppermute | solution.py:487
  123.3 6.9 %copy-start.5 = (f32[512,1024]{1,0:T(8,128)S(1)}, f32[512,1024]{1,0:T(8,128)}, u32[]{:S(2)}) copy-start(f32[512,1024]{1,0:T(8,128)} %refs_6_.3) | copy-start | bytes 6291460
  123.4 6.9 %copy-start.6 = (f32[512,1024]{1,0:T(8,128)S(1)}, f32[512,1024]{1,0:T(8,128)}, u32[]{:S(2)}) copy-start(f32[512,1024]{1,0:T(8,128)} %refs_7_.3) | copy-start | bytes 6291460
  (8 other events, 7.3 us)

commit v3 on v2

--- a/solution.py
+++ b/solution.py
@@ -262,11 +262,27 @@
     )(own, other, own, other, *[w] * len(which))
 
 
-def weights_kernel(y_ref, obs_ref, joined_ref, o0, o1, o2, o3, acc, blocks):
+def weights_kernel(y_ref, obs_hbm, joined_hbm, o0, o1, o2, o3, acc, blocks, obs_v, joined_v, sems):
     step = pl.program_id(0)
-    joined = joined_ref[...]
+
+    def loads(i):
+        rows = pl.ds(pl.multiple_of(i * CHUNK, CHUNK), CHUNK)
+        return (
+            pltpu.make_async_copy(obs_hbm.at[rows], obs_v.at[i], sems.at[0, i]),
+            pltpu.make_async_copy(joined_hbm.at[rows], joined_v.at[i], sems.at[1, i]),
+        )
+
+    @pl.when(step == 0)
+    def _():
+        for i in range(obs_v.shape[0]):
+            for load in loads(i):
+                load.start()
+
+    for load in loads(step):
+        load.wait()
+    joined = joined_v[step]
     j_hi, j_lo = split(joined)
-    o_hi, o_lo = split(obs_ref[...])
+    o_hi, o_lo = split(obs_v[step])
     value = mm(j_hi, o_hi, 0, 0) + mm(j_lo, o_hi, 0, 0) + mm(j_hi, o_lo, 0, 0)
 
     @pl.when(step == 0)
@@ -295,12 +311,15 @@
         grid=(tok // CHUNK,),
         in_specs=[
             SCALARS,
-            pl.BlockSpec((CHUNK, width), lambda i: (i, 0)),
-            pl.BlockSpec((CHUNK, 2 * DH), lambda i: (i, 0)),
+            HBM, HBM,
         ],
         out_specs=[pl.BlockSpec((nz, own, 2 * DH), lambda i: (0, 0, 0))] * NY,
         out_shape=[shape(nz, own, 2 * DH)] * NY,
-        scratch_shapes=[VMEM((2 * DH, width), F32), VMEM((nz, NY, own, 2 * DH), F32)],
+        scratch_shapes=[
+            VMEM((2 * DH, width), F32), VMEM((nz, NY, own, 2 * DH), F32),
+            VMEM((tok // CHUNK, CHUNK, width), F32), VMEM((tok // CHUNK, CHUNK, 2 * DH), F32),
+            pltpu.SemaphoreType.DMA((2, tok // CHUNK)),
+        ],
         compiler_params=params(60),
         cost_estimate=cost(tok * width * 2 * DH, 11 << 20),
         name="weight_grads",
@@ -398,15 +417,20 @@
         out_ref[i, :, 5 * DH :] = weights[half:]
 
 
-def gathered_kernel(got_ref, rows_ref, key_ref, value_ref):
+def gathered_kernel(got_ref, rows_ref):
+    half = got_ref.shape[1]
+    for i in range(got_ref.shape[0]):
+        rows_ref[i * half : (i + 1) * half] = got_ref[i, :, : 3 * DH]
+
+
+def weight_sum_kernel(mark_ref, got_ref, key_ref, value_ref, next_ref):
     half = got_ref.shape[1]
     total = got_ref[0, :, 3 * DH :]
     for i in range(1, got_ref.shape[0]):
         total += got_ref[i, :, 3 * DH :]
-    for i in range(got_ref.shape[0]):
-        rows_ref[i * half : (i + 1) * half] = got_ref[i, :, : 3 * DH]
     key_ref[:half], key_ref[half:] = total[:, :DH], total[:, 2 * DH : 3 * DH]
     value_ref[:half], value_ref[half:] = total[:, DH : 2 * DH], total[:, 3 * DH :]
+    next_ref[...] = mark_ref[...]
 
 
 def final_kernel(y_ref, _, own, r1, r2, r3, lat_ref, dout_ref, d_lat_ref, d_wq_ref, d_wo_ref, all_rows):
@@ -479,15 +503,18 @@
     )
     from_left_2 = lax.ppermute(right_2, "head", right)
     from_right_2 = lax.ppermute(left_2, "head", left)
-    rows, d_w_key, d_w_value = small_call(
-        gathered_kernel,
-        [shape(rows_y, 3 * DH), shape(width // n_ctx, DH), shape(width // n_ctx, DH)],
-        [got], [], name="gathered",
+    (rows,) = small_call(
+        gathered_kernel, [shape(rows_y, 3 * DH)], [got], [], name="gathered"
     )
     rows = [rows] + [lax.ppermute(rows, "ctx", along_y(k)) for k in range(1, NY)]
     d_observations, mark = small_call(
         last_kernel, [shape(2 * half, DH), shape(8, DH)],
         [home, from_left_1, from_right_1, from_left_2, from_right_2], [], name="token_last",
+    )
+    d_w_key, d_w_value, mark = small_call(
+        weight_sum_kernel,
+        [shape(width // n_ctx, DH), shape(width // n_ctx, DH), shape(8, DH)],
+        [mark, got], [], name="weight_sum",
     )
     d_latents, d_w_query, d_w_out = small_call(
         final_kernel, [shape(lat, DH), shape(width, DH), shape(DH, width)],

time: 135 us -> 134 us (level)
  waiting for transfers between devices: 24.7 us -> 22.8 us
    ppermute x3, waiting for transfers between devices: 4.06 us -> 2.16 us  [on_device(): lax.ppermute(rows, 'ctx', along_y(k))]
    pallas_call x6 -> x7, Pallas kernels: 10.5 us -> 11.5 us  [small_call(): pl.pallas_call(body, in_specs=[ANY] * len(after) + [SCALARS] * len(scalar...]
  transfers between devices with their start and end apart: 16 -> 16, of which waited for: 6 -> 5; matrix products, arithmetic and copies ran while one was open for 0% -> 0% of each run, Pallas kernels for 20% -> 20%
where the time goes in v3:
time: 134 us; the launch traced here: 132 us
  Pallas kernels  53.6 us (40%)
  starting transfers between devices  45.7 us (34%)
  waiting for transfers between devices  22.8 us (17%)
  local copies, waits for them, and re-layouts  8.92 us (7%)
    pallas_call x1, Pallas kernels, forward(): pl.pallas_call(lambda *refs: forward_kernel(1.0 / math.sqrt(DH), *refs),...  14.6 us
    pallas_call x7, Pallas kernels, small_call(): pl.pallas_call(body, in_specs=[ANY] * len(after) + [SCALARS] * len(scalar...  11.5 us
    pallas_call x1, Pallas kernels, token_grads(): pl.pallas_call(lambda *refs: grads_kernel(1.0 / math.sqrt(DH), *refs), gr...  9.79 us
    all_to_all x1, waiting for transfers between devices, on_device(): stats = lax.all_to_all(sent, 'ctx', 0, 0)  9.59 us
    all_to_all x1, starting transfers between devices, on_device(): stats = lax.all_to_all(sent, 'ctx', 0, 0)  9.47 us
    unnamed x32, local copies, waits for them, and re-layouts  8.92 us
    pallas_call x2, Pallas kernels, token_part(): pl.pallas_call(kernel, grid=(steps,), in_specs=[a, a, b, b] + chosen, out...  8.09 us
    pallas_call x1, Pallas kernels, weight_grads(): pl.pallas_call(weights_kernel, grid=(tok // CHUNK,), in_specs=[SCALARS, H...  7.57 us
  transfers between devices with their start and end apart: 16, of which 5 were waited for; matrix products, arithmetic and copies ran while one was open for 0% of the time, Pallas kernels for 20%

profile of v3, /device:TPU:1, one launch (start us, length us, event | category | flops | bytes accessed | tf_op | source)
XLA Modules:
  0.0 131.9 jit_solution(17303556400777657588)
XLA Ops:
  0.7 14.6 %forward.1 = (bf16[2048,512]{1,0:T(8,128)(2,1)}, bf16[512,384]{1,0:T(8,128)(2,1)}, bf16[512,384]{1,0:T(8,128)(2,1)}, f32[32,3,512]{2,1,0:T(4,128)}, f32[3,512]{1,0:T(4,128)}, /*index=5*/f32[4,128,256]{2,1,0:T(8,128)}) custom-call(s32[1]{0:T(128)} %bitcast.2.refs_0_, f32[512,1024]{1,0:T(8,128)} %refs_6_.3, f32[512,1024]{1,0:T(8,128)} %refs_7_.3, ...), custom_call_target="tpu_custom_call" | custom-call | flops 4831838208 | bytes 18874368 | tf_op jit(solution)/shard_map/forward/pallas_call | solution.py:146
  15.2 3.3 %collective-permute-start = (f32[4,128,256]{2,1,0:T(8,128)}, f32[4,128,256]{2,1,0:T(8,128)S(1)}, u32[]{:S(2)}, u32[]{:S(2)}) collective-permute-start(f32[4,128,256]{2,1,0:T(8,128)} %get-tuple-element.36), channel_id=1, source_target_pairs={{0,1},{1,0},{2,3},{3,2},{4,5},{5,4},{6,7},{7,6},{8,9},{9,8},{10,11... | collective-permute-start | bytes 1572872 | tf_op jit(solution)/shard_map/ppermute | solution.py:468
  18.6 9.5 %all-to-all-start = ((f32[32,3,512]{2,1,0:T(4,128)}), f32[32,3,512]{2,1,0:T(4,128)S(1)}, u32[]{:S(2)}, u32[]{:S(2)}) async-start(f32[32,3,512]{2,1,0:T(4,128)} %get-tuple-element.38), calls=%async_computation | async-start | bytes 524288 | tf_op jit(solution)/shard_map/all_to_all | solution.py:467
  30.4 9.6 %all-to-all-done.refs_1_ = f32[32,3,512]{2,1,0:T(4,128)S(1)} async-done(((f32[32,3,512]{2,1,0:T(4,128)}), f32[32,3,512]{2,1,0:T(4,128)S(1)}, u32[]{:S(2)}, u32[]{:S(2)}) %all-to-all-start) | async-done | bytes 196640 | tf_op jit(solution)/shard_map/all_to_all | solution.py:467
  40.7 9.8 %token_grads.1 = (f32[2048,256]{1,0:T(8,128)}, f32[512,256]{1,0:T(8,128)}) custom-call(f32[8,128]{1,0:T(8,128)} %copy-done.14, f32[32,3,512]{2,1,0:T(4,128)} %copy-done.15, bf16[2048,512]{1,0:T(8,128)(2,1)} %get-tuple-element.39.refs_2_, bf16[512,384]{1,0:T(8,128)(2,1)} %get-tuple-element.40.refs_3_, bf16[512,384]{1,0:T(8,128)(2,1)} %get-tuple-element.41.refs_4_), custom_call_target="tpu_custom_call" | custom-call | flops 4831838208 | bytes 6291456 | tf_op jit(solution)/shard_map/token_grads/pallas_call | solution.py:204
  50.5 2.0 %collective-permute-start.1 = (f32[2048,256]{1,0:T(8,128)}, f32[2048,256]{1,0:T(8,128)S(1)}, u32[]{:S(2)}, u32[]{:S(2)}) collective-permute-start(f32[2048,256]{1,0:T(8,128)} %get-tuple-element.42.own_a.own_b.joined_hbm), channel_id=1, source_target_pairs={{0,1},{1,0},{2,3},{3,2},{4,5},{5,4},{6,7},{7,6},{8,9},{9,8},{10,11... | collective-permute-start | bytes 6291464 | tf_op jit(solution)/shard_map/ppermute | solution.py:476
  52.5 4.6 %all-to-all-start.1 = ((f32[32,16,256]{2,1,0:T(8,128)}), f32[32,16,256]{2,1,0:T(8,128)}, u32[]{:S(2)}, u32[]{:S(2)}) async-start(f32[32,16,256]{2,1,0:T(8,128)} %bitcast.4), calls=%async_computation.1 | async-start | bytes 1048576 | tf_op jit(solution)/shard_map/all_to_all | solution.py:477
  58.5 5.5 %token_first.1 = (f32[2,1024,128]{2,1,0:T(8,128)}, f32[2,1024,128]{2,1,0:T(8,128)}) custom-call(f32[2048,256]{1,0:T(8,128)} %get-tuple-element.42.own_a.own_b.joined_hbm, f32[2048,256]{1,0:T(8,128)} %copy-done.3, f32[2048,256]{1,0:T(8,128)} %get-tuple-element.42.own_a.own_b.joined_hbm, f32[2048,256]{1,0:T(8,128)} %copy-done.3, bf16[4,256,512]{2,1,0:T(8,128)(2,1)} %copy-done, ...), custom_call_target="tpu_custom_call" | custom-call | flops 1610612736 | bytes 6291456 | tf_op jit(solution)/shard_map/token_first/pallas_call | solution.py:253
  66.7 7.6 %weight_grads.1 = (f32[8,32,256]{2,1,0:T(8,128)}, f32[8,32,256]{2,1,0:T(8,128)}, f32[8,32,256]{2,1,0:T(8,128)}, f32[8,32,256]{2,1,0:T(8,128)}) custom-call(s32[1]{0:T(128)} %bitcast.y_ref.refs_0_, f32[2048,1024]{1,0:T(8,128)} %obs_hbm.1, f32[2048,256]{1,0:T(8,128)} %get-tuple-element.42.own_a.own_b.joined_hbm), custom_call_target="tpu_custom_call" | custom-call | flops 3221225472 | bytes 11534336 | tf_op jit(solution)/shard_map/weight_grads/pallas_call | solution.py:309
  75.5 2.4 %collective-permute-start.7 = (f32[8,32,256]{2,1,0:T(8,128)}, f32[8,32,256]{2,1,0:T(8,128)}, u32[]{:S(2)}, u32[]{:S(2)}) collective-permute-start(f32[8,32,256]{2,1,0:T(8,128)} %get-tuple-element.57), channel_id=1, source_target_pairs={{0,16},{8,24},{16,0},{24,8},{32,48},{40,56},{48,32},{56,40},{64,80... | collective-permute-start | bytes 786440 | tf_op jit(solution)/shard_map/ppermute | solution.py:479
  80.1 2.0 %latent_part.1 = (f32[16,256]{1,0:T(8,128)S(1)}, f32[8,16,128]{2,1,0:T(8,128)}) custom-call(f32[32,16,256]{2,1,0:T(8,128)} %all-to-all-done.1.refs_0_, f32[1024,128]{1,0:T(8,128)S(1)} %copy-done.12), custom_call_target="tpu_custom_call" | custom-call | flops 6291456 | bytes 1048576 | tf_op jit(solution)/shard_map/latent_part/pallas_call | solution.py:362
  82.2 4.9 %all-to-all-start.2 = ((f32[8,16,128]{2,1,0:T(8,128)}), f32[8,16,128]{2,1,0:T(8,128)S(1)}, u32[]{:S(2)}, u32[]{:S(2)}) async-start(f32[8,16,128]{2,1,0:T(8,128)} %get-tuple-element.54), calls=%async_computation.2 | async-start | bytes 131072 | tf_op jit(solution)/shard_map/all_to_all | solution.py:494
  87.0 2.3 %collective-permute-done.7.refs_4_ = f32[8,32,256]{2,1,0:T(8,128)} collective-permute-done((f32[8,32,256]{2,1,0:T(8,128)}, f32[8,32,256]{2,1,0:T(8,128)}, u32[]{:S(2)}, u32[]{:S(2)}) %collective-permute-start.7) | collective-permute-done | bytes 262176 | tf_op jit(solution)/shard_map/ppermute | solution.py:479
  89.4 2.5 %all-to-all-done.2.refs_1_ = f32[8,16,128]{2,1,0:T(8,128)S(1)} async-done(((f32[8,16,128]{2,1,0:T(8,128)}), f32[8,16,128]{2,1,0:T(8,128)S(1)}, u32[]{:S(2)}, u32[]{:S(2)}) %all-to-all-start.2) | async-done | bytes 65568 | tf_op jit(solution)/shard_map/all_to_all | solution.py:494
  94.7 6.5 %all-to-all-start.3 = ((f32[8,16,896]{2,1,0:T(8,128)}), f32[8,16,896]{2,1,0:T(8,128)}, u32[]{:S(2)}, u32[]{:S(2)}) async-start(f32[8,16,896]{2,1,0:T(8,128)} %copy-done.7), calls=%async_computation.3 | async-start | bytes 917504 | tf_op jit(solution)/shard_map/all_to_all | solution.py:499
  102.8 2.6 %token_rest.1 = (f32[1024,128]{1,0:T(8,128)S(1)}, f32[1024,128]{1,0:T(8,128)S(1)}, f32[2,1024,128]{2,1,0:T(8,128)S(1)}) custom-call(f32[2048,256]{1,0:T(8,128)S(1)} %copy-done.2, f32[2048,256]{1,0:T(8,128)S(1)} %copy-done.4, f32[2048,256]{1,0:T(8,128)S(1)} %copy-done.2, f32[2048,256]{1,0:T(8,128)S(1)} %copy-done.4, bf16[4,256,512]{2,1,0:T(8,128)(2,1)S(1)} %copy-done.1, ...), custom_call_target="tpu_custom_call" | custom-call | flops 1610612736 | bytes 6291456 | tf_op jit(solution)/shard_map/token_rest/pallas_call | solution.py:253
  106.4 1.7 %token_second.1 = (f32[1024,128]{1,0:T(8,128)S(1)}, f32[1024,128]{1,0:T(8,128)S(1)}) custom-call(f32[1024,128]{1,0:T(8,128)S(1)} %get-tuple-element.47.refs_0_, f32[1024,128]{1,0:T(8,128)S(1)} %get-tuple-element.48.refs_1_, f32[2,1024,128]{2,1,0:T(8,128)} %collective-permute-done.2.refs_2_.refs_1_, f32[2,1024,128]{2,1,0:T(8,128)} %collective-permute-done.3.refs_3_.refs_2_), custom_call_target="tpu_custom_call" | custom-call | flops 6291456 | bytes 1048576 | tf_op jit(solution)/shard_map/token_second/pallas_call | solution.py:333
  108.9 2.0 %collective-permute-start.5 = (f32[1024,128]{1,0:T(8,128)S(1)}, f32[1024,128]{1,0:T(8,128)S(1)}, u32[]{:S(2)}, u32[]{:S(2)}) collective-permute-start(f32[1024,128]{1,0:T(8,128)S(1)} %get-tuple-element.50), channel_id=1, source_target_pairs={{0,6},{1,7},{2,0},{3,1},{4,2},{5,3},{6,4},{7,5},{8,14},{9,15},{10,... | collective-permute-start | bytes 1572872 | tf_op jit(solution)/shard_map/ppermute | solution.py:505
  110.9 6.1 %all-to-all-done.3.refs_1_.refs_0_ = f32[8,16,896]{2,1,0:T(8,128)} async-done(((f32[8,16,896]{2,1,0:T(8,128)}), f32[8,16,896]{2,1,0:T(8,128)}, u32[]{:S(2)}, u32[]{:S(2)}) %all-to-all-start.3) | async-done | bytes 458784 | tf_op jit(solution)/shard_map/all_to_all | solution.py:499
  119.2 2.4 %collective-permute-start.10 = (f32[128,384]{1,0:T(8,128)S(1)}, f32[128,384]{1,0:T(8,128)S(1)}, u32[]{:S(2)}, u32[]{:S(2)}) collective-permute-start(f32[128,384]{1,0:T(8,128)S(1)} %gathered.1.refs_2_), channel_id=1, source_target_pairs={{0,16},{8,24},{16,0},{24,8},{32,48},{40,56},{48,32},{56,40},{64,80... | collective-permute-start | bytes 589832 | tf_op jit(solution)/shard_map/ppermute | solution.py:509
  122.8 2.8 %token_last.1 = (f32[2048,128]{1,0:T(8,128)}, f32[8,128]{1,0:T(8,128)S(1)}) custom-call(f32[2,1024,128]{2,1,0:T(8,128)S(1)} %copy-done.9, f32[2,1024,128]{2,1,0:T(8,128)} %collective-permute-done.2.refs_2_.refs_1_, f32[2,1024,128]{2,1,0:T(8,128)} %collective-permute-done.3.refs_3_.refs_2_, f32[1024,128]{1,0:T(8,128)S(1)} %collective-permute-done.4.refs_3_, ...), custom_call_target="tpu_custom_call" | custom-call | flops 6291456 | bytes 1048576 | tf_op jit(solution)/shard_map/token_last/pallas_call | solution.py:333
  125.6 1.6 %weight_sum.1 = (f32[32,128]{1,0:T(8,128)}, f32[32,128]{1,0:T(8,128)}, f32[8,128]{1,0:T(8,128)S(1)}) custom-call(f32[8,128]{1,0:T(8,128)S(1)} %get-tuple-element.51.refs_0_, f32[8,16,896]{2,1,0:T(8,128)} %all-to-all-done.3.refs_1_.refs_0_), custom_call_target="tpu_custom_call" | custom-call | flops 6291456 | bytes 1048576 | tf_op jit(solution)/shard_map/weight_sum/pallas_call | solution.py:333
  127.3 2.2 %collective-permute-done.10.refs_4_ = f32[128,384]{1,0:T(8,128)S(1)} collective-permute-done((f32[128,384]{1,0:T(8,128)S(1)}, f32[128,384]{1,0:T(8,128)S(1)}, u32[]{:S(2)}, u32[]{:S(2)}) %collective-permute-start.10) | collective-permute-done | bytes 196640 | tf_op jit(solution)/shard_map/ppermute | solution.py:509
  129.4 2.5 %final.1 = (f32[512,128]{1,0:T(8,128)}, f32[1024,128]{1,0:T(8,128)}, f32[128,1024]{1,0:T(8,128)}) custom-call(s32[1]{0:T(128)} %bitcast.y_ref.refs_0_, f32[8,128]{1,0:T(8,128)S(1)} %get-tuple-element.59.refs_1_, f32[128,384]{1,0:T(8,128)S(1)} %gathered.1.refs_2_, f32[128,384]{1,0:T(8,128)S(1)} %collective-permute-done.9.refs_3_, ...), custom_call_target="tpu_custom_call" | custom-call | flops 6291456 | bytes 1048576 | tf_op jit(solution)/shard_map/final/pallas_call | solution.py:333
  (54 shorter events, 20.0 us)
Async XLA Ops:
  0.6 27.5 %copy-start.10 = (f32[1024,128]{1,0:T(8,128)S(1)}, f32[1024,128]{1,0:T(8,128)}, u32[]{:S(2)}) copy-start(f32[1024,128]{1,0:T(8,128)} %refs_1_.4) | copy-start | bytes 1572868
  0.7 27.5 %copy-start.11 = (f32[1024,128]{1,0:T(8,128)S(1)}, f32[1024,128]{1,0:T(8,128)}, u32[]{:S(2)}) copy-start(f32[1024,128]{1,0:T(8,128)} %refs_2_.3) | copy-start | bytes 1572868
  15.2 12.9 %collective-permute-start = (f32[4,128,256]{2,1,0:T(8,128)}, f32[4,128,256]{2,1,0:T(8,128)S(1)}, u32[]{:S(2)}, u32[]{:S(2)}) collective-permute-start(f32[4,128,256]{2,1,0:T(8,128)} %get-tuple-element.36), channel_id=1, source_target_pairs={{0,1},{1,0},{2,3},{3,2},{4,5},{5,4},{6,7},{7,6},{8,9},{9,8},{10,11... | collective-permute-start | bytes 1572872 | tf_op jit(solution)/shard_map/ppermute | solution.py:468
  18.6 21.5 %all-to-all-start = ((f32[32,3,512]{2,1,0:T(4,128)}), f32[32,3,512]{2,1,0:T(4,128)S(1)}, u32[]{:S(2)}, u32[]{:S(2)}) async-start(f32[32,3,512]{2,1,0:T(4,128)} %get-tuple-element.38), calls=%async_computation | async-start | bytes 524288 | tf_op jit(solution)/shard_map/all_to_all | solution.py:467
  50.5 6.6 %collective-permute-start.1 = (f32[2048,256]{1,0:T(8,128)}, f32[2048,256]{1,0:T(8,128)S(1)}, u32[]{:S(2)}, u32[]{:S(2)}) collective-permute-start(f32[2048,256]{1,0:T(8,128)} %get-tuple-element.42.own_a.own_b.joined_hbm), channel_id=1, source_target_pairs={{0,1},{1,0},{2,3},{3,2},{4,5},{5,4},{6,7},{7,6},{8,9},{9,8},{10,11... | collective-permute-start | bytes 6291464 | tf_op jit(solution)/shard_map/ppermute | solution.py:476
  52.5 26.5 %all-to-all-start.1 = ((f32[32,16,256]{2,1,0:T(8,128)}), f32[32,16,256]{2,1,0:T(8,128)}, u32[]{:S(2)}, u32[]{:S(2)}) async-start(f32[32,16,256]{2,1,0:T(8,128)} %bitcast.4), calls=%async_computation.1 | async-start | bytes 1048576 | tf_op jit(solution)/shard_map/all_to_all | solution.py:477
  64.0 42.4 %collective-permute-start.2 = (f32[2,1024,128]{2,1,0:T(8,128)}, f32[2,1024,128]{2,1,0:T(8,128)}, u32[]{:S(2)}, u32[]{:S(2)}) collective-permute-start(f32[2,1024,128]{2,1,0:T(8,128)} %get-tuple-element.45), channel_id=1, source_target_pairs={{0,2},{1,3},{2,4},{3,5},{4,6},{5,7},{6,0},{7,1},{8,10},{9,11},{10,... | collective-permute-start | bytes 3145736 | tf_op jit(solution)/shard_map/ppermute | solution.py:483
  65.2 41.2 %collective-permute-start.3 = (f32[2,1024,128]{2,1,0:T(8,128)}, f32[2,1024,128]{2,1,0:T(8,128)}, u32[]{:S(2)}, u32[]{:S(2)}) collective-permute-start(f32[2,1024,128]{2,1,0:T(8,128)} %get-tuple-element.46), channel_id=1, source_target_pairs={{0,6},{1,7},{2,0},{3,1},{4,2},{5,3},{6,4},{7,5},{8,14},{9,15},{10,... | collective-permute-start | bytes 3145736 | tf_op jit(solution)/shard_map/ppermute | solution.py:484
  74.3 26.9 %copy-start.1 = (bf16[4,256,512]{2,1,0:T(8,128)(2,1)S(1)}, bf16[4,256,512]{2,1,0:T(8,128)(2,1)}, u32[]{:S(2)}) copy-start(bf16[4,256,512]{2,1,0:T(8,128)(2,1)} %copy-done) | copy-start | bytes 3145732
  74.3 26.9 %copy-start.2 = (f32[2048,256]{1,0:T(8,128)S(1)}, f32[2048,256]{1,0:T(8,128)}, u32[]{:S(2)}) copy-start(f32[2048,256]{1,0:T(8,128)} %get-tuple-element.42.own_a.own_b.joined_hbm) | copy-start | bytes 6291460
  74.3 12.7 %collective-permute-start.6 = (f32[8,32,256]{2,1,0:T(8,128)}, f32[8,32,256]{2,1,0:T(8,128)S(1)}, u32[]{:S(2)}, u32[]{:S(2)}) collective-permute-start(f32[8,32,256]{2,1,0:T(8,128)} %get-tuple-element.56), channel_id=1, source_target_pairs={{0,8},{8,16},{16,24},{24,0},{32,40},{40,48},{48,56},{56,32},{64,72... | collective-permute-start | bytes 786440 | tf_op jit(solution)/shard_map/ppermute | solution.py:479
  75.5 13.9 %collective-permute-start.7 = (f32[8,32,256]{2,1,0:T(8,128)}, f32[8,32,256]{2,1,0:T(8,128)}, u32[]{:S(2)}, u32[]{:S(2)}) collective-permute-start(f32[8,32,256]{2,1,0:T(8,128)} %get-tuple-element.57), channel_id=1, source_target_pairs={{0,16},{8,24},{16,0},{24,8},{32,48},{40,56},{48,32},{56,40},{64,80... | collective-permute-start | bytes 786440 | tf_op jit(solution)/shard_map/ppermute | solution.py:479
  77.9 11.5 %collective-permute-start.8 = (f32[8,32,256]{2,1,0:T(8,128)}, f32[8,32,256]{2,1,0:T(8,128)}, u32[]{:S(2)}, u32[]{:S(2)}) collective-permute-start(f32[8,32,256]{2,1,0:T(8,128)} %get-tuple-element.58), channel_id=1, source_target_pairs={{0,24},{8,0},{16,8},{24,16},{32,56},{40,32},{48,40},{56,48},{64,88... | collective-permute-start | bytes 786440 | tf_op jit(solution)/shard_map/ppermute | solution.py:479
  82.2 9.8 %all-to-all-start.2 = ((f32[8,16,128]{2,1,0:T(8,128)}), f32[8,16,128]{2,1,0:T(8,128)S(1)}, u32[]{:S(2)}, u32[]{:S(2)}) async-start(f32[8,16,128]{2,1,0:T(8,128)} %get-tuple-element.54), calls=%async_computation.2 | async-start | bytes 131072 | tf_op jit(solution)/shard_map/all_to_all | solution.py:494
  94.7 22.3 %all-to-all-start.3 = ((f32[8,16,896]{2,1,0:T(8,128)}), f32[8,16,896]{2,1,0:T(8,128)}, u32[]{:S(2)}, u32[]{:S(2)}) async-start(f32[8,16,896]{2,1,0:T(8,128)} %copy-done.7), calls=%async_computation.3 | async-start | bytes 917504 | tf_op jit(solution)/shard_map/all_to_all | solution.py:499
  101.2 1.6 %copy-start.4 = (f32[2048,256]{1,0:T(8,128)S(1)}, f32[2048,256]{1,0:T(8,128)}, u32[]{:S(2)}) copy-start(f32[2048,256]{1,0:T(8,128)} %copy-done.3) | copy-start | bytes 6291460
  106.4 16.4 %copy-start.9 = (f32[2,1024,128]{2,1,0:T(8,128)S(1)}, f32[2,1024,128]{2,1,0:T(8,128)}, u32[]{:S(2)}) copy-start(f32[2,1024,128]{2,1,0:T(8,128)} %copy-done.8) | copy-start | bytes 3145732
  108.2 14.6 %collective-permute-start.4 = (f32[1024,128]{1,0:T(8,128)S(1)}, f32[1024,128]{1,0:T(8,128)S(1)}, u32[]{:S(2)}, u32[]{:S(2)}) collective-permute-start(f32[1024,128]{1,0:T(8,128)S(1)} %get-tuple-element.49), channel_id=1, source_target_pairs={{0,2},{1,3},{2,4},{3,5},{4,6},{5,7},{6,0},{7,1},{8,10},{9,11},{10,... | collective-permute-start | bytes 1572872 | tf_op jit(solution)/shard_map/ppermute | solution.py:504
  108.9 13.8 %collective-permute-start.5 = (f32[1024,128]{1,0:T(8,128)S(1)}, f32[1024,128]{1,0:T(8,128)S(1)}, u32[]{:S(2)}, u32[]{:S(2)}) collective-permute-start(f32[1024,128]{1,0:T(8,128)S(1)} %get-tuple-element.50), channel_id=1, source_target_pairs={{0,6},{1,7},{2,0},{3,1},{4,2},{5,3},{6,4},{7,5},{8,14},{9,15},{10,... | collective-permute-start | bytes 1572872 | tf_op jit(solution)/shard_map/ppermute | solution.py:505
  118.1 9.2 %collective-permute-start.9 = (f32[128,384]{1,0:T(8,128)S(1)}, f32[128,384]{1,0:T(8,128)S(1)}, u32[]{:S(2)}, u32[]{:S(2)}) collective-permute-start(f32[128,384]{1,0:T(8,128)S(1)} %gathered.1.refs_2_), channel_id=1, source_target_pairs={{0,8},{8,16},{16,24},{24,0},{32,40},{40,48},{48,56},{56,32},{64,72... | collective-permute-start | bytes 589832 | tf_op jit(solution)/shard_map/ppermute | solution.py:509
  119.2 10.2 %collective-permute-start.10 = (f32[128,384]{1,0:T(8,128)S(1)}, f32[128,384]{1,0:T(8,128)S(1)}, u32[]{:S(2)}, u32[]{:S(2)}) collective-permute-start(f32[128,384]{1,0:T(8,128)S(1)} %gathered.1.refs_2_), channel_id=1, source_target_pairs={{0,16},{8,24},{16,0},{24,8},{32,48},{40,56},{48,32},{56,40},{64,80... | collective-permute-start | bytes 589832 | tf_op jit(solution)/shard_map/ppermute | solution.py:509
  121.6 7.8 %collective-permute-start.11 = (f32[128,384]{1,0:T(8,128)S(1)}, f32[128,384]{1,0:T(8,128)S(1)}, u32[]{:S(2)}, u32[]{:S(2)}) collective-permute-start(f32[128,384]{1,0:T(8,128)S(1)} %gathered.1.refs_2_), channel_id=1, source_target_pairs={{0,24},{8,0},{16,8},{24,16},{32,56},{40,32},{48,40},{56,48},{64,88... | collective-permute-start | bytes 589832 | tf_op jit(solution)/shard_map/ppermute | solution.py:509
  122.8 6.6 %copy-start.5 = (f32[512,1024]{1,0:T(8,128)S(1)}, f32[512,1024]{1,0:T(8,128)}, u32[]{:S(2)}) copy-start(f32[512,1024]{1,0:T(8,128)} %refs_6_.3) | copy-start | bytes 6291460
  122.8 6.6 %copy-start.6 = (f32[512,1024]{1,0:T(8,128)S(1)}, f32[512,1024]{1,0:T(8,128)}, u32[]{:S(2)}) copy-start(f32[512,1024]{1,0:T(8,128)} %refs_7_.3) | copy-start | bytes 6291460
  (8 other events, 7.3 us)
